TPU v7x, 32 devices: a whole 2x2x4 slice. The times are simulated.
32 devices in a mesh: rep: 2 (over x), sp: 16 (over z, y, core).
Axes of the slice: x: 2, y: 2, z: 4, core: 2. Of those that a mesh axis runs over, the one named last changes fastest.
Arguments:
- volume: bfloat16 [128, 16, 16, 128], P(('rep', 'sp')), parts along dimension 0, may hold values from -6 to 6
- first_kernel: bfloat16 [3, 3, 3, 128, 128], replicated, may hold values from -0.15625 to 0.15625
- second_kernel: bfloat16 [3, 3, 3, 128, 256], replicated, may hold values from -0.15625 to 0.15625
- deep_kernel: bfloat16 [3, 3, 3, 256, 512], P(None, None, None, None, 'sp'), may hold values from -0.109375 to 0.109375
- deeper_kernel: bfloat16 [3, 3, 3, 512, 512], P(None, None, None, None, 'sp'), may hold values from -0.078125 to 0.078125
- rise_kernel: bfloat16 [2, 2, 2, 512, 256], replicated, may hold values from -0.375 to 0.375
- decode_kernel: bfloat16 [3, 3, 3, 512, 256], P(None, None, None, 'sp'), may hold values from -0.078125 to 0.078125
- final_kernel: bfloat16 [2, 2, 2, 256, 128], replicated, may hold values from -0.5 to 0.5
Outputs:
- segmented: bfloat16 [128, 16, 16, 128], P(('rep', 'sp')), parts along dimension 0
There are 2 independent parts, one for each index of `rep`. A program takes and returns all parts, laid end to end along the dimension named above; an argument that names none is the same for every part. Nothing has to cross between parts.
All inputs are finite; a program needn't handle non-finite values.
Results may differ from a plain program's by a relative error of at most 0.015.
Values may be sent and summed in bfloat16 or wider, within the bound.
No kernel may reach another device: no remote copies, remote signals or barrier semaphores. Data moves between devices by JAX's collectives and lax.ppermute only.
A program may use at most 64 MiB of HBM per device.

v0:
```python
import functools

import jax
import jax.numpy as jnp
import numpy as np
from jax import lax
from jax.experimental import pallas as pl
from jax.experimental.pallas import tpu as pltpu
from jax.sharding import PartitionSpec as P

GROUP = 4
MIB = 1024 * 1024


def call(kernel, outs, scratch, args, flops, vmem_mib, scalars=0, unread=0):
    spaces = [pltpu.SMEM] * scalars + [pltpu.VMEM] * (len(args) - scalars - unread)
    spaces += [pl.ANY] * unread
    return pl.pallas_call(
        kernel,
        out_shape=outs,
        in_specs=[pl.BlockSpec(memory_space=space) for space in spaces],
        out_specs=jax.tree.map(lambda _: pl.BlockSpec(memory_space=pltpu.VMEM), outs),
        scratch_shapes=scratch,
        compiler_params=pltpu.CompilerParams(vmem_limit_bytes=vmem_mib * MIB),
        cost_estimate=pl.CostEstimate(
            flops=flops,
            bytes_accessed=sum(a.size * a.dtype.itemsize for a in args[: len(args) - unread]),
            transcendentals=0,
        ),
    )(*args)


def dot(left, right, dims=((1,), (0,))):
    return lax.dot_general(left, right, (dims, ((), ())), preferred_element_type=jnp.float32)


def round_once(values):
    return values.astype(jnp.bfloat16).astype(jnp.float32)


def fill_patches(framed, patches, slices):
    for b in range(3):
        for c in range(3):
            tap = framed[:, b : b + 8, 7 + c : 15 + c, :].reshape(slices * 64, 128)
            col = (b * 3 + c) * 128
            patches[:, col : col + 128] = tap.astype(jnp.bfloat16)


def shift_slice(shifted, s, values):
    row = lax.broadcasted_iota(jnp.int32, (256, 128), 0) & 15
    here = values.reshape(256, 128).astype(jnp.float32)
    before = jnp.where(row == 0, 0.0, pltpu.roll(here, 1, 0))
    after = jnp.where(row == 15, 0.0, pltpu.roll(here, 255, 0))
    shifted[s, 0] = jnp.zeros((16, 384), jnp.bfloat16)
    shifted[s, 17] = jnp.zeros((16, 384), jnp.bfloat16)
    for c, tap in enumerate((before, here, after)):
        tap = tap.astype(jnp.bfloat16).reshape(16, 16, 128)
        shifted[s, 1:17, :, 128 * c : 128 * c + 128] = tap


def depth_pair(shifted, slices, weights, steps):
    left = jnp.concatenate(
        [shifted[s, b : b + 16].reshape(256, 384) for s in slices for b in range(3)], axis=1
    )
    none = jnp.zeros((1152, 128), jnp.bfloat16)
    right = [
        jnp.concatenate(
            [weights[j] if j < 3 else none, weights[j - 1] if j > 0 else none], axis=1
        )
        for j in steps
    ]
    return dot(left, jnp.concatenate(right, axis=0))


def depth_one(shifted, s, weights):
    left = jnp.concatenate([shifted[s, b : b + 16].reshape(256, 384) for b in range(3)], axis=1)
    return dot(left, weights)


def front_stage(odd, rep, volume, decode, off_chip, on_chip, *refs):
    done = refs[-1]
    pairs = [
        (volume.at[pl.ds(odd[0], 3)], off_chip),
        (volume.at[pl.ds(1 - odd[0], 3)], on_chip),
    ]
    if len(refs) == 2:
        block = refs[0]
        at = pl.multiple_of(528 * rep[0], 16)
        pairs += [
            (decode.at[pl.ds(at, 336)], block.at[pl.ds(0, 336)]),
            (decode.at[pl.ds(336, 192)], block.at[pl.ds(336, 192)]),
        ]
    copies = [
        pltpu.make_async_copy(source, target, done.at[i]) for i, (source, target) in enumerate(pairs)
    ]
    for copy in copies:
        copy.start()
    for copy in copies:
        copy.wait()


def own_stage(volume, weights, out, shifted):
    for s in range(4):
        shift_slice(shifted, s, volume[s])
    out[0, :, :128] = jnp.zeros((256, 128), jnp.float32)
    out[0, :, 128:] = depth_one(shifted, 0, weights[2])
    out[1] = depth_pair(shifted, (0, 1, 2), weights, (1, 2, 3))
    out[2] = depth_pair(shifted, (1, 2, 3), weights, (0, 1, 2))
    out[3, :, :128] = depth_one(shifted, 3, weights[0])
    out[3, :, 128:] = jnp.zeros((256, 128), jnp.float32)


def stem_stage(marks, off_chip, on_chip, own, weights, second, order, _, *refs):
    pooled_out, skip_outs = refs[0], refs[1 : 1 + GROUP]
    shifted, halves, framed, patches, quarters, blocks = refs[1 + GROUP :]
    for s in range(3):
        even = marks[4] == 0
        shift_slice(shifted, s, jnp.where(even, off_chip[s], on_chip[s]))
        shift_slice(shifted, 3 + s, jnp.where(even, on_chip[s], off_chip[s]))
    framed[...] = jnp.zeros(framed.shape, jnp.float32)
    for m in range(4):
        if m == 0:
            first = own[0] + depth_pair(shifted, (0, 1, 2), weights, (0, 1, 2))
        elif m == 3:
            first = own[3] + depth_pair(shifted, (3, 4, 5), weights, (1, 2, 3))
        elif m == 1:
            near = own[1, :, :128] + depth_one(shifted, 2, weights[0])
            first = jnp.concatenate([near, own[1, :, 128:]], axis=1)
        else:
            far = own[2, :, 128:] + depth_one(shifted, 3, weights[2])
            first = jnp.concatenate([own[2, :, :128], far], axis=1)
        first = round_once(jnp.maximum(first, 0.0))
        pair = (first[:, :128] + first[:, 128:]).reshape(8, 32, 128)
        halves[...] = (pair[:, :16] + pair[:, 16:]).reshape(128, 128)
        pooled = halves[pl.ds(0, 64, stride=2), :] + halves[pl.ds(1, 64, stride=2), :]
        pooled = round_once(pooled * 0.125)
        if m == 0:
            pooled = jnp.where(marks[5] == 0, 0.0, pooled)
        if m == 3:
            pooled = jnp.where(marks[6] == 0, 0.0, pooled)
        framed[m, 1:9, 8:16, :] = pooled.reshape(8, 8, 128)
    fill_patches(framed, patches, 4)
    skip = dot(patches[0:128], second[0])
    skip += dot(patches[64:192], second[1])
    skip += dot(patches[128:256], second[2])
    skip = jnp.maximum(skip, 0.0).astype(jnp.bfloat16)
    wide = skip.astype(jnp.float32)
    pair = (wide[:64] + wide[64:]).reshape(4, 16, 256)
    pair = (pair[:, :8] + pair[:, 8:]).reshape(32, 256)
    for k in range(2):
        quarters[k] = pair[:, 128 * k : 128 * k + 128]
    pooled = jnp.concatenate(
        [
            quarters[k, pl.ds(0, 16, stride=2), :] + quarters[k, pl.ds(1, 16, stride=2), :]
            for k in range(2)
        ],
        axis=1,
    )
    pooled = (pooled * 0.125).astype(jnp.bfloat16)
    for p in range(pooled_out.shape[0]):
        pooled_out[p] = pooled
    sorted_skip = dot(skip, order[...])
    for r in range(GROUP):
        near, far = sorted_skip[:64, 64 * r : 64 * r + 64], sorted_skip[64:, 64 * r : 64 * r + 64]
        block = jnp.concatenate([near, far], axis=1)
        block = jnp.concatenate([block[:32], block[32:]], axis=1).astype(jnp.bfloat16)
        blocks[r, 0:32, :] = block
        first, last = sorted_skip[16 * r : 16 * r + 16], sorted_skip[64 + 16 * r : 80 + 16 * r]
        blocks[r, 32:48, :] = jnp.where(marks[0] == 0, first, last).astype(jnp.bfloat16)
    for k in range(GROUP):
        skip_outs[k][...] = blocks[marks[0] ^ k]


def edge_slice(block, far):
    lower = lax.broadcasted_iota(jnp.int32, (16, 128), 1) < 64
    sides = []
    for k in range(2):
        half = block[:, 128 * k : 128 * k + 128].astype(jnp.float32)
        top, bottom = half[:16], half[16:]
        if far:
            top = pltpu.roll(top, 64, 1)
        else:
            bottom = pltpu.roll(bottom, 64, 1)
        sides.append(jnp.where(lower, top, bottom))
    return jnp.concatenate(sides, axis=1)


def spread_taps(weights, values, dims, chans, voxels):
    lane = lax.broadcasted_iota(jnp.int32, (chans, voxels), 1)

    def moved(term, tap, step, place, last):
        if tap == 1:
            return term
        keep = place > 0 if tap == 0 else place < last
        return jnp.where(keep, pltpu.roll(term, ((1 - tap) * step) % voxels, 1), 0.0)

    total = None
    for a in range(3):
        products = dot(weights[a * 9 * chans : (a + 1) * 9 * chans, :], values, dims)
        plane = None
        for b in range(3):
            line = None
            for c in range(3):
                at = (b * 3 + c) * chans
                term = moved(products[at : at + chans], c, 1, lane & 3, 3)
                line = term if line is None else line + term
            line = moved(line, b, 4, (lane >> 2) & 3, 3)
            plane = line if plane is None else plane + line
        plane = moved(plane, a, 16, lane >> 4, voxels // 16 - 1)
        total = plane if total is None else total + plane
    return jnp.maximum(total, 0.0)


def by_rank(marks, near, blocks):
    for k in range(GROUP):
        blocks[marks[0] ^ k] = near[k][near[k].shape[0] - 48 :, :]


def by_depth(marks, near, parts, step):
    for k in range(GROUP):
        parts[marks[0] ^ k] = near[k][0 : parts.shape[1], :]
    return jnp.concatenate(
        [
            parts[r, at : at + step, :]
            for at in range(0, parts.shape[1], step)
            for r in range(GROUP)
        ],
        axis=0,
    )


def relay_stage(marks, *refs):
    line, refs = refs[:GROUP], refs[GROUP:]
    step = line[0].shape[0]
    skips, outs = refs[:GROUP], refs[GROUP:]
    for j in range(GROUP):
        for k in range(GROUP):
            outs[j][pl.ds(pl.multiple_of((marks[3] ^ k) * step, 16), step), :] = line[k][...]
        outs[j][GROUP * step :, :] = skips[j][...]


def edge_stage(marks, *refs):
    near, (near_swap, far_swap, blocks) = refs[:GROUP], refs[GROUP:]
    by_rank(marks, near, blocks)
    first = edge_slice(blocks[0, 0:32, :], False)
    last = edge_slice(blocks[GROUP - 1, 0:32, :], True)
    even = marks[2] == 0
    near_swap[...] = jnp.where(even, last, first).astype(jnp.bfloat16)
    far_swap[...] = jnp.where(even, first, last).astype(jnp.bfloat16)


def deep_stage(marks, weights, *refs):
    near, out, parts = refs[:-2], refs[-2], refs[-1]
    _, chans, voxels = out.shape
    values = near[0][...] if len(near) == 1 else by_depth(marks, near, parts, 16)
    deep = spread_taps(weights, values, ((1,), (1,)), chans, voxels).astype(jnp.bfloat16)
    for dest in range(out.shape[0]):
        out[dest] = deep


def deeper_stage(near_count, marks, weights, *refs):
    near, (deep, out, blocks) = refs[:near_count], refs[near_count:]
    n, chans, _ = out.shape
    voxels = deep.shape[1]
    deeper = spread_taps(weights, deep[...], ((1,), (0,)), chans, voxels)
    lane = lax.broadcasted_iota(jnp.int32, (chans, 128), 1)
    planes = n // GROUP
    ride = len(near) == GROUP
    if ride:
        by_rank(marks, near, blocks)
        edges = [blocks[r, 32:48, :].astype(jnp.float32) for r in (0, GROUP - 1)]
        riders = [
            [
                jnp.concatenate(
                    [
                        pltpu.roll(edge[:, at // 128 * 128 : at // 128 * 128 + 128], (96 - at) % 128, 1)
                        for at in (64 * r, 64 * r + 32)
                    ],
                    axis=0,
                )
                for r in range(GROUP)
            ]
            for edge in edges
        ]
    for p in range(planes):
        part = pltpu.roll(deeper, (16 - 64 * p) % voxels, 1)[:, :128]
        if p == 0:
            part = jnp.where(lane < 16, 0.0, part)
        if p == planes - 1:
            part = jnp.where(lane >= 80, 0.0, part)
        for r in range(GROUP):
            whole = part
            if ride:
                rider = jnp.where(marks[3] < p, riders[1][r], riders[0][r])
                whole = jnp.where(lane < 96, part, rider)
            out[GROUP * p + r] = whole.astype(jnp.bfloat16)


def rise_stage(marks, chans, rise, out):
    lane = lax.broadcasted_iota(jnp.int32, (256, 64), 1)
    row = lax.broadcasted_iota(jnp.int32, (256, 64), 0)
    source = (marks[0] + GROUP * (lane // chans)) * chans + lane % chans
    mine = jnp.where(row == source, 1.0, 0.0).astype(jnp.bfloat16)
    for pair in range(4):
        both = [dot(rise[2 * pair + k], mine) for k in range(2)]
        both = jnp.concatenate(both, axis=1).astype(jnp.bfloat16)
        out[:, 128 * pair : 128 * pair + 128] = both


def decode_stage(ride, marks, deeper, rise, *refs):
    swaps = () if ride else refs[:2]
    near, refs = refs[len(swaps) : len(swaps) + GROUP], refs[len(swaps) + GROUP :]
    decode, outs = refs[: -5 - GROUP], refs[-5 - GROUP : -5]
    framed, patches, risen, blocks, parts = refs[-5:]
    by_rank(marks, near, blocks)
    n, chans, _ = deeper.shape
    plane, planes = marks[3], n // GROUP
    upper = lax.broadcasted_iota(jnp.int32, (64, 128), 1) >= 64

    def edge(low):
        if not ride:
            even = marks[2] == 0
            sides = [swap[...].astype(jnp.float32) for swap in swaps]
            side = jnp.where(even, sides[low], sides[not low])
            parts = []
            for k in range(2):
                half = side[:, 128 * k : 128 * k + 128]
                parts += [pltpu.roll(half, 64, 1), half]
            return jnp.concatenate(parts, axis=0)
        other = jnp.maximum(plane - 1, 0) if low else jnp.minimum(plane + 1, planes - 1)
        lane = lax.broadcasted_iota(jnp.int32, (16, 128), 1)
        parts = []
        for r in range(GROUP):
            block = deeper[GROUP * other + r].astype(jnp.float32)
            parts.append(jnp.where(lane < 96, pltpu.roll(block[:16], 96, 1), block[16:]))
        return jnp.where(other == plane, 0.0, jnp.concatenate(parts, axis=0))

    framed[...] = jnp.zeros(framed.shape, jnp.float32)
    spread = round_once(dot(deeper[...].reshape(n * chans, 128).astype(jnp.float32).T.astype(jnp.bfloat16), rise[...]))
    for pair in range(4):
        both = spread[:, 128 * pair : 128 * pair + 128]
        risen[2 * pair] = both
        risen[2 * pair + 1] = pltpu.roll(both, 64, 1)
    for s in range(10):
        d, a = (s + 1) // 2, (s + 1) % 2
        for h in range(4):
            for b in range(2):
                for c in range(2):
                    framed[s, 1 + 2 * h + b, pl.ds(8 + c, 4, stride=2), :] = risen[
                        4 * a + 2 * b + c, 16 * d + 4 * h : 16 * d + 4 * h + 4, :
                    ]
        if s == 0 or s == 9:
            skip = edge(s == 0)
        else:
            both = blocks[(s - 1) // 2, 0:32, :].astype(jnp.float32)
            skip = jnp.concatenate([both[:, :128], both[:, 128:]], axis=0)
            if (s - 1) % 2 == 0:
                skip = pltpu.roll(skip, 64, 1)
        joined = framed[s, 1:9, 8:16, :].reshape(64, 128)
        framed[s, 1:9, 8:16, :] = jnp.where(upper, skip, joined).reshape(8, 8, 128)
    fill_patches(framed, patches, 10)
    def rows_at(rep, z, row):
        if rep == 0 and row >= 528:
            return decode[1][z, row - 528 : row - 512, :]
        if rep == 1 and row < 336:
            return decode[1][z, row : row + 16, :]
        if rep == 1 and row >= 528:
            row -= 528
        return decode[0][z, row : row + 16, :]

    def multiply(rep):
        count = decode[0].shape[0]
        step = 128 // count
        partial = None
        for a in range(3):
            right = [
                rows_at(rep, z, row)
                for tap in range(9 * a, 9 * a + 9)
                for z in range(count)
                for row in range(tap * step, (tap + 1) * step, 16)
            ]
            term = dot(patches[64 * a : 64 * a + 512], jnp.concatenate(right, axis=0))
            partial = term if partial is None else partial + term
        parts[...] = partial.astype(jnp.bfloat16).reshape(GROUP, 128, 256)

    if len(decode) == 1:
        multiply(None)
    else:
        pl.when(marks[1] == 0)(lambda: multiply(0))
        pl.when(marks[1] == 1)(lambda: multiply(1))
    for k in range(GROUP):
        outs[k][...] = parts[marks[0] ^ k]


def final_stage(*refs):
    partials, (weights, out, spaced) = refs[:GROUP], refs[GROUP:]
    decoded = partials[0][...].astype(jnp.float32)
    for partial in partials[1:]:
        decoded += partial[...].astype(jnp.float32)
    decoded = jnp.maximum(decoded, 0.0).astype(jnp.bfloat16)
    for a in range(2):
        for b in range(2):
            for c in range(2):
                values = dot(decoded, weights[4 * a + 2 * b + c])
                for d in range(2):
                    for h in range(8):
                        at = ((2 * d + a) * 16 + 2 * h + b) * 16 + c
                        spaced[pl.ds(at, 8, stride=2), :] = values[64 * d + 8 * h : 64 * d + 8 * h + 8]
    out[...] = spaced[...].astype(jnp.bfloat16)


ALL = ("z", "r")


def exchange(payload, axis):
    return lax.all_to_all(payload, axis, split_axis=0, concat_axis=0, tiled=True)


def by_xor(blocks, axis):
    swaps = [[(r, r ^ k) for r in range(GROUP)] for k in range(GROUP)]
    return [blocks[0]] + [lax.ppermute(blocks[k], axis, swaps[k]) for k in range(1, GROUP)]


def body(
    volume,
    first_kernel,
    second_kernel,
    deep_kernel,
    deeper_kernel,
    rise_kernel,
    decode_kernel,
    final_kernel,
):
    n = lax.axis_size(ALL)
    place = lax.axis_index(ALL)
    planes = n // GROUP
    rank = lax.axis_index("r")
    chans = deep_kernel.shape[4]
    voxels = 16 * n
    bf16 = functools.partial(jax.ShapeDtypeStruct, dtype=jnp.bfloat16)

    rep, plane = lax.axis_index("rep"), lax.axis_index("z")
    marks = jnp.stack([rank, rep, plane % 2, plane, place % 2, place, n - 1 - place])
    marks = marks.astype(jnp.int32)
    decode_block = decode_kernel.reshape(27 * chans, 256)
    shared = lax.axis_size("rep") == 2 and chans == 32
    ride = chans == 32
    paired = planes == GROUP
    halo = bf16((3, 16, 16, 128))
    in_spaces = [pltpu.SMEM, pltpu.SMEM, pl.ANY, pl.ANY]
    off_chip, on_chip, *share = pl.pallas_call(
        front_stage,
        out_shape=(halo, halo) + (bf16((528, 256)),) * shared,
        in_specs=[pl.BlockSpec(memory_space=space) for space in in_spaces],
        out_specs=(pl.BlockSpec(memory_space=pltpu.VMEM),) * (2 + shared),
        scratch_shapes=[pltpu.SemaphoreType.DMA((4,))],
        compiler_params=pltpu.CompilerParams(vmem_limit_bytes=60 * MIB),
        cost_estimate=pl.CostEstimate(flops=0, bytes_accessed=10**6, transcendentals=0),
    )(
        (place % 2).astype(jnp.int32).reshape(1),
        rep.astype(jnp.int32).reshape(1),
        volume,
        decode_block,
    )
    pairs = [(i, i + 1) for i in range(1, n - 1, 2)]
    off_chip = lax.ppermute(off_chip, ALL, pairs + [(j, i) for i, j in pairs])
    on_chip = lax.ppermute(on_chip, ALL, [(i, i ^ 1) for i in range(n)])
    if shared:
        decode_block = share[0]
    line = lax.all_gather(decode_block, "z", axis=0)

    pairs = [(i, i + 1) for i in range(1, n - 1, 2)]
    taps = first_kernel.reshape(3, 1152, 128)
    own = call(
        own_stage,
        jax.ShapeDtypeStruct((4, 256, 256), jnp.float32),
        [pltpu.VMEM((4, 18, 16, 384), jnp.bfloat16)],
        (volume, taps),
        2 * 1024 * 2304 * 256,
        24,
    )
    lane = np.arange(256)
    source = (lane // 64 + GROUP * (lane % 64 // chans)) * chans + lane % chans
    order = jnp.asarray(np.arange(256)[:, None] == source[None, :], jnp.bfloat16)
    rise_part = call(
        lambda marks_ref, *refs: rise_stage(marks_ref, chans, *refs),
        bf16((n * chans, 512)),
        [],
        (marks, rise_kernel.reshape(8, n * chans, 256)),
        2 * 8 * n * chans * 256 * 64,
        16,
        scalars=1,
    )
    pooled_two, *skips = call(
        stem_stage,
        (bf16((1 if paired else n, 16, 256)),) + (bf16((48, 256)),) * GROUP,
        [
            pltpu.VMEM((6, 18, 16, 384), jnp.bfloat16),
            pltpu.VMEM((128, 128), jnp.float32),
            pltpu.VMEM((4, 10, 24, 128), jnp.float32),
            pltpu.VMEM((256, 1152), jnp.bfloat16),
            pltpu.VMEM((2, 32, 128), jnp.float32),
            pltpu.VMEM((GROUP, 48, 256), jnp.bfloat16),
        ],
        (marks, off_chip, on_chip, own, taps, second_kernel.reshape(3, 1152, 256), order, rise_part),
        2 * 1024 * 2304 * 256,
        24,
        scalars=1,
        unread=1,
    )
    if paired:
        line_blocks = by_xor([pooled_two.reshape(16, 256)] * GROUP, "z")
        relays = call(
            relay_stage,
            (bf16((112, 256)),) * GROUP,
            [],
            (marks, *line_blocks, *skips),
            0,
            16,
            scalars=1,
        )
        near = by_xor(relays, "r")
        pooled_whole = near
    else:
        pooled_whole = (exchange(pooled_two, ALL).reshape(voxels, 256),)
        near = by_xor(skips, "r")
    blocks = pltpu.VMEM((GROUP, 48, 256), jnp.bfloat16)

    deep = call(
        deep_stage,
        bf16((n, chans, voxels)),
        [pltpu.VMEM((GROUP, 64, 256), jnp.bfloat16)],
        (
            marks,
            deep_kernel.transpose(0, 1, 2, 4, 3).reshape(27 * chans, 256),
            *pooled_whole,
        ),
        2 * 27 * chans * 256 * voxels,
        16,
        scalars=1,
    )
    if shared:
        first_row = (deep[0, 0, 0] < 0).astype(jnp.int32)
        piece = lax.dynamic_slice_in_dim(line, first_row, 336, axis=1)
        weights = (line, lax.ppermute(piece, "rep", [(0, 1), (1, 0)]))
    elif chans % 16:
        weights = line.reshape(planes, 27, chans, 256).transpose(1, 0, 2, 3)
        weights = (weights.reshape(1, 27 * 128, 256),)
    else:
        weights = (line,)
    swaps = ()
    if not ride:
        swaps = call(
            edge_stage,
            (bf16((16, 256)), bf16((16, 256))),
            [blocks],
            (marks, *near),
            0,
            16,
            scalars=1,
        )
        near_pairs = [(p, p + 1) for p in range(0, planes - 1, 2)]
        far_pairs = [(p, p + 1) for p in range(1, planes - 1, 2)]
        near_swap = lax.ppermute(swaps[0], "z", near_pairs + [(j, i) for i, j in near_pairs])
        far_swap = lax.ppermute(swaps[1], "z", far_pairs + [(j, i) for i, j in far_pairs])
        swaps = (near_swap, far_swap)
    deep_whole = (exchange(deep, ALL).reshape(n * chans, voxels),)

    riders = near if ride else ()
    deeper = call(
        functools.partial(deeper_stage, len(riders)),
        bf16((n, chans, 128)),
        [blocks],
        (
            marks,
            deeper_kernel.transpose(0, 1, 2, 4, 3).reshape(27 * chans, n * chans),
            *riders,
            *deep_whole,
        ),
        2 * 27 * chans * n * chans * voxels,
        16,
        scalars=1,
    )
    deeper_near = exchange(deeper, ALL)

    partials = call(
        functools.partial(decode_stage, ride),
        (bf16((128, 256)),) * GROUP,
        [
            pltpu.VMEM((10, 10, 24, 128), jnp.float32),
            pltpu.VMEM((640, 1152), jnp.bfloat16),
            pltpu.VMEM((8, 128, 128), jnp.float32),
            blocks,
            pltpu.VMEM((GROUP, 128, 256), jnp.bfloat16),
        ],
        (marks, deeper_near, rise_part, *swaps, *near, *weights),
        2 * 512 * 3456 * 256,
        24,
        scalars=1,
    )
    partials = by_xor(partials, "r")
    out = call(
        final_stage,
        bf16((1024, 128)),
        [pltpu.VMEM((1024, 128), jnp.float32)],
        (*partials, final_kernel.reshape(8, 256, 128)),
        2 * 128 * 256 * 1024,
        16,
    )
    return out.reshape(4, 16, 16, 128)


def solution(mesh):
    reps, n = mesh.devices.shape
    grid = jax.sharding.Mesh(mesh.devices.reshape(reps, n // GROUP, GROUP), ("rep",) + ALL)
    return jax.shard_map(
        body,
        mesh=grid,
        in_specs=(
            P(("rep",) + ALL, None, None, None),
            P(),
            P(),
            P(None, None, None, None, ALL),
            P(None, None, None, None, ALL),
            P(),
            P(None, None, None, ALL, None),
            P(),
        ),
        out_specs=P(("rep",) + ALL, None, None, None),
        check_vma=False,
    )
```

profile of v0, /device:TPU:1, one launch (start us, length us, event | category | flops | bytes accessed | tf_op | source)
XLA Modules:
  0.0 81.9 jit_solution(16812085293930013822)
XLA Ops:
  6.5 2.1 %shard_map.91 = (bf16[3,16,16,128]{3,2,1,0:T(8,128)(2,1)}, bf16[3,16,16,128]{3,2,1,0:T(8,128)(2,1)}, bf16[528,256]{1,0:T(8,128)(2,1)}) custom-call(s32[1]{0:T(128)} %bitcast.4.odd, s32[1]{0:T(128)} %bitcast.1.rep, bf16[4,16,16,128]{3,2,1,0:T(8,128)(2,1)} %volume.3, bf16[864,256]{1,0:T(8,128)(2,1)} %bitcast.37), custom_call_target="tpu_custom_call" | custom-call | bytes 1000000 | tf_op jit(solution)/shard_map/pallas_call | solution.py:451
  8.7 4.5 %collective-permute-start = (bf16[3,16,16,128]{3,2,1,0:T(8,128)(2,1)}, bf16[3,16,16,128]{3,2,1,0:T(8,128)(2,1)S(1)}, u32[]{:S(2)}, u32[]{:S(2)}) collective-permute-start(bf16[3,16,16,128]{3,2,1,0:T(8,128)(2,1)} %get-tuple-element.21), channel_id=1, source_target_pairs={{1,2},{3,4},{5,6},{7,8},{9,10},{11,12},{13,14},{2,1},{4,3},{6,5},{... | collective-permute-start | bytes 589832 | tf_op jit(solution)/shard_map/ppermute | solution.py:466
  13.4 1.6 %copy-done = bf16[2,2,2,512,256]{4,3,2,1,0:T(8,128)(2,1)S(1)} copy-done((bf16[2,2,2,512,256]{4,3,2,1,0:T(8,128)(2,1)S(1)}, bf16[2,2,2,512,256]{4,3,2,1,0:T(8,128)(2,1)}, u32[]{:S(2)}) %copy-start) | copy-done | bytes 2097176
  15.0 1.3 %shard_map.93._.rise = bf16[512,512]{1,0:T(8,128)(2,1)S(1)} custom-call(s32[7]{0:T(128)S(1)} %stack.31.marks_ref.marks, bf16[8,512,256]{2,1,0:T(8,128)(2,1)S(1)} %bitcast.23), custom_call_target="tpu_custom_call" | custom-call | flops 134217728 | bytes 2097180 | tf_op jit(solution)/shard_map/pallas_call | solution.py:18
  16.4 1.4 %shard_map.92.own = f32[4,256,256]{2,1,0:T(8,128)S(1)} custom-call(bf16[4,16,16,128]{3,2,1,0:T(8,128)(2,1)S(1)} %copy-done.7, bf16[3,1152,128]{2,1,0:T(8,128)(2,1)S(1)} %bitcast.26), custom_call_target="tpu_custom_call" | custom-call | flops 1207959552 | bytes 1146880 | tf_op jit(solution)/shard_map/pallas_call | solution.py:18
  17.8 0.4 collective-permute-done.off_chip
  18.3 2.9 %shard_map.94 = (bf16[1,16,256]{2,1,0:T(8,128)(2,1)S(1)}, bf16[48,256]{1,0:T(8,128)(2,1)S(1)}, bf16[48,256]{1,0:T(8,128)(2,1)S(1)}, bf16[48,256]{1,0:T(8,128)(2,1)S(1)}, bf16[48,256]{1,0:T(8,128)(2,1)S(1)}) custom-call(s32[7]{0:T(128)S(1)} %stack.31.marks_ref.marks, bf16[3,16,16,128]{3,2,1,0:T(8,128)(2,1)S(1)} %collective-permute-done.off_chip, ...), custom_call_target="tpu_custom_call" | custom-call | flops 1207959552 | bytes 4227100 | tf_op jit(solution)/shard_map/pallas_call | solution.py:18
  21.2 4.0 %collective-permute-start.4 = (bf16[16,256]{1,0:T(8,128)(2,1)S(1)}, bf16[16,256]{1,0:T(8,128)(2,1)S(1)}, u32[]{:S(2)}, u32[]{:S(2)}) collective-permute-start(bf16[16,256]{1,0:T(8,128)(2,1)S(1)} %bitcast.33), channel_id=1, source_target_pairs={{0,12},{4,8},{8,4},{12,0},{1,13},{5,9},{9,5},{13,1},{2,14},{6,10},... | collective-permute-start | bytes 24584 | tf_op jit(solution)/shard_map/ppermute | solution.py:421
  25.2 0.4 collective-permute-start.2
  25.6 1.0 %collective-permute-done.4.refs_3_ = bf16[16,256]{1,0:T(8,128)(2,1)S(1)} collective-permute-done((bf16[16,256]{1,0:T(8,128)(2,1)S(1)}, bf16[16,256]{1,0:T(8,128)(2,1)S(1)}, u32[]{:S(2)}, u32[]{:S(2)}) %collective-permute-start.4) | collective-permute-done | bytes 8224 | tf_op jit(solution)/shard_map/ppermute | solution.py:421
  26.5 2.8 %collective-permute-done.3.refs_2_ = bf16[16,256]{1,0:T(8,128)(2,1)S(1)} collective-permute-done((bf16[16,256]{1,0:T(8,128)(2,1)S(1)}, bf16[16,256]{1,0:T(8,128)(2,1)S(1)}, u32[]{:S(2)}, u32[]{:S(2)}) %collective-permute-start.3) | collective-permute-done | bytes 8224 | tf_op jit(solution)/shard_map/ppermute | solution.py:421
  29.3 0.6 shard_map.95
  29.9 0.5 collective-permute-start.5
  30.4 1.3 %collective-permute-start.6 = (bf16[112,256]{1,0:T(8,128)(2,1)S(1)}, bf16[112,256]{1,0:T(8,128)(2,1)S(1)}, u32[]{:S(2)}, u32[]{:S(2)}) collective-permute-start(bf16[112,256]{1,0:T(8,128)(2,1)S(1)} %get-tuple-element.30), channel_id=1, source_target_pairs={{0,2},{1,3},{2,0},{3,1},{4,6},{5,7},{6,4},{7,5},{8,10},{9,11},{10,... | collective-permute-start | bytes 172040 | tf_op jit(solution)/shard_map/ppermute | solution.py:421
  31.6 0.5 collective-permute-start.7
  32.1 1.9 %collective-permute-done.6.refs_2_ = bf16[112,256]{1,0:T(8,128)(2,1)S(1)} collective-permute-done((bf16[112,256]{1,0:T(8,128)(2,1)S(1)}, bf16[112,256]{1,0:T(8,128)(2,1)S(1)}, u32[]{:S(2)}, u32[]{:S(2)}) %collective-permute-start.6) | collective-permute-done | bytes 57376 | tf_op jit(solution)/shard_map/ppermute | solution.py:421
  34.0 1.9 %collective-permute-done.7.refs_3_ = bf16[112,256]{1,0:T(8,128)(2,1)S(1)} collective-permute-done((bf16[112,256]{1,0:T(8,128)(2,1)S(1)}, bf16[112,256]{1,0:T(8,128)(2,1)S(1)}, u32[]{:S(2)}, u32[]{:S(2)}) %collective-permute-start.7) | collective-permute-done | bytes 57376 | tf_op jit(solution)/shard_map/ppermute | solution.py:421
  35.9 1.8 %shard_map.96 = bf16[16,32,256]{2,1,0:T(8,128)(2,1)} custom-call(s32[7]{0:T(128)S(1)} %stack.31.marks_ref.marks, bf16[864,256]{1,0:T(8,128)(2,1)S(1)} %bitcast.30, bf16[112,256]{1,0:T(8,128)(2,1)S(1)} %get-tuple-element.28.refs_0_, bf16[112,256]{1,0:T(8,128)(2,1)S(1)} %collective-permute-done.5.refs_1_, bf16[112,256]{1,0:T(8,128)(2,1)S(1)} %collective-permute-done.6.refs_2_, ...), custom_call_target="tpu_custom_call" | custom-call | flops 113246208 | bytes 671772 | tf_op jit(solution)/shard_map/pallas_call | solution.py:18
  37.7 1.3 %slice.4 = bf16[1,1,1]{2,1,0:T(2,128)(2,1)} slice(bf16[16,32,256]{2,1,0:T(8,128)(2,1)} %shard_map.96), slice={[0:1], [0:1], [0:1]} | slice | bytes 4 | tf_op jit(solution)/shard_map/slice | solution.py:543
  39.0 4.5 %all-to-all-start = ((bf16[16,32,256]{2,1,0:T(8,128)(2,1)}), bf16[16,32,256]{2,1,0:T(8,128)(2,1)S(1)}, u32[]{:S(2)}, u32[]{:S(2)}) async-start(bf16[16,32,256]{2,1,0:T(8,128)(2,1)} %shard_map.96), calls=%async_computation | async-start | bytes 524288 | tf_op jit(solution)/shard_map/all_to_all | solution.py:416
  44.3 2.2 %constant_dynamic-slice_fusion = bf16[4,336,256]{2,1,0:T(8,128)(2,1)} fusion(bf16[4,528,256]{2,1,0:T(8,128)(2,1)} %bitcast.31, s32[]{:T(128)S(6)} %select_n.18), kind=kLoop, calls=%fused_computation | loop fusion | bytes 1376260 | tf_op jit(solution)/shard_map/dynamic_slice | solution.py:544
  46.5 1.2 %collective-permute-start.8 = (bf16[4,336,256]{2,1,0:T(8,128)(2,1)}, bf16[4,336,256]{2,1,0:T(8,128)(2,1)}, u32[]{:S(2)}, u32[]{:S(2)}) collective-permute-start(bf16[4,336,256]{2,1,0:T(8,128)(2,1)} %constant_dynamic-slice_fusion), channel_id=1, source_target_pairs={{0,16},{16,0},{1,17},{17,1},{2,18},{18,2},{3,19},{19,3},{4,20},{20... | collective-permute-start | bytes 2064392 | tf_op jit(solution)/shard_map/ppermute | solution.py:545
  47.7 5.3 %all-to-all-done = bf16[16,32,256]{2,1,0:T(8,128)(2,1)S(1)} async-done(((bf16[16,32,256]{2,1,0:T(8,128)(2,1)}), bf16[16,32,256]{2,1,0:T(8,128)(2,1)S(1)}, u32[]{:S(2)}, u32[]{:S(2)}) %all-to-all-start) | async-done | bytes 262176 | tf_op jit(solution)/shard_map/all_to_all | solution.py:416
  53.0 1.3 %shard_map.97 = bf16[16,32,128]{2,1,0:T(8,128)(2,1)S(1)} custom-call(s32[7]{0:T(128)S(1)} %stack.31.marks_ref.marks, bf16[864,512]{1,0:T(8,128)(2,1)S(1)} %bitcast.28, bf16[112,256]{1,0:T(8,128)(2,1)S(1)} %get-tuple-element.28.refs_0_, bf16[112,256]{1,0:T(8,128)(2,1)S(1)} %collective-permute-done.5.refs_1_, ...), custom_call_target="tpu_custom_call" | custom-call | flops 226492416 | bytes 1376284 | tf_op jit(solution)/shard_map/pallas_call | solution.py:18
  54.3 10.3 %all_to_all.10.deeper = bf16[16,32,128]{2,1,0:T(8,128)(2,1)S(1)} all-to-all(bf16[16,32,128]{2,1,0:T(8,128)(2,1)S(1)} %shard_map.97), channel_id=1, replica_groups=mesh['rep'=2,'z'=4,'r'=4] {'z','r'}, dimensions={0} | all-to-all | bytes 262144 | tf_op jit(solution)/shard_map/all_to_all | solution.py:416
  64.6 2.9 %shard_map.98 = (bf16[128,256]{1,0:T(8,128)(2,1)S(1)}, bf16[128,256]{1,0:T(8,128)(2,1)S(1)}, bf16[128,256]{1,0:T(8,128)(2,1)S(1)}, bf16[128,256]{1,0:T(8,128)(2,1)S(1)}) custom-call(s32[7]{0:T(128)S(1)} %stack.31.marks_ref.marks, bf16[16,32,128]{2,1,0:T(8,128)(2,1)S(1)} %all_to_all.10.deeper, bf16[512,512]{1,0:T(8,128)(2,1)S(1)} %shard_map.93._.rise, ...), custom_call_target="tpu_custom_call" | custom-call | flops 905969664 | bytes 2654236 | tf_op jit(solution)/shard_map/pallas_call | solution.py:18
  67.5 1.2 %collective-permute-start.9 = (bf16[128,256]{1,0:T(8,128)(2,1)S(1)}, bf16[128,256]{1,0:T(8,128)(2,1)S(1)}, u32[]{:S(2)}, u32[]{:S(2)}) collective-permute-start(bf16[128,256]{1,0:T(8,128)(2,1)S(1)} %get-tuple-element.34), channel_id=1, source_target_pairs={{0,1},{1,0},{2,3},{3,2},{4,5},{5,4},{6,7},{7,6},{8,9},{9,8},{10,11... | collective-permute-start | bytes 196616 | tf_op jit(solution)/shard_map/ppermute | solution.py:421
  68.8 0.3 collective-permute-start.10
  69.0 1.5 %collective-permute-start.11 = (bf16[128,256]{1,0:T(8,128)(2,1)S(1)}, bf16[128,256]{1,0:T(8,128)(2,1)S(1)}, u32[]{:S(2)}, u32[]{:S(2)}) collective-permute-start(bf16[128,256]{1,0:T(8,128)(2,1)S(1)} %get-tuple-element.36), channel_id=1, source_target_pairs={{0,3},{1,2},{2,1},{3,0},{4,7},{5,6},{6,5},{7,4},{8,11},{9,10},{10,... | collective-permute-start | bytes 196616 | tf_op jit(solution)/shard_map/ppermute | solution.py:421
  70.5 2.0 %collective-permute-done.10.refs_2_ = bf16[128,256]{1,0:T(8,128)(2,1)S(1)} collective-permute-done((bf16[128,256]{1,0:T(8,128)(2,1)S(1)}, bf16[128,256]{1,0:T(8,128)(2,1)S(1)}, u32[]{:S(2)}, u32[]{:S(2)}) %collective-permute-start.10) | collective-permute-done | bytes 65568 | tf_op jit(solution)/shard_map/ppermute | solution.py:421
  72.5 1.6 %collective-permute-done.11.refs_3_ = bf16[128,256]{1,0:T(8,128)(2,1)S(1)} collective-permute-done((bf16[128,256]{1,0:T(8,128)(2,1)S(1)}, bf16[128,256]{1,0:T(8,128)(2,1)S(1)}, u32[]{:S(2)}, u32[]{:S(2)}) %collective-permute-start.11) | collective-permute-done | bytes 65568 | tf_op jit(solution)/shard_map/ppermute | solution.py:421
  74.0 1.1 %shard_map.99 = bf16[1024,128]{1,0:T(8,128)(2,1)} custom-call(bf16[128,256]{1,0:T(8,128)(2,1)S(1)} %get-tuple-element.33.refs_0_, bf16[128,256]{1,0:T(8,128)(2,1)S(1)} %collective-permute-done.9.refs_1_, bf16[128,256]{1,0:T(8,128)(2,1)S(1)} %collective-permute-done.10.refs_2_, bf16[128,256]{1,0:T(8,128)(2,1)S(1)} %collective-permute-done.11.refs_3_, ...), custom_call_target="tpu_custom_call" | custom-call | flops 67108864 | bytes 786432 | tf_op jit(solution)/shard_map/pallas_call | solution.py:18
  (28 shorter events, 0.3 us)
Async XLA Ops:
  6.5 37.7 %all-gather.3.cloned.1.call-start = ((), (), s32[]{:S(2)}) async-start(), calls=%async_computation.2 | async-start | bytes 1351680 | tf_op jit(solution)/shard_map/all_gather | solution.py:470
  6.5 9.8 %copy-start.2 = (bf16[3,3,3,128,128]{4,3,2,1,0:T(8,128)(2,1)S(1)}, bf16[3,3,3,128,128]{4,3,2,1,0:T(8,128)(2,1)}, u32[]{:S(2)}) copy-start(bf16[3,3,3,128,128]{4,3,2,1,0:T(8,128)(2,1)} %param.10) | copy-start | bytes 2654212
  8.7 9.6 %collective-permute-start = (bf16[3,16,16,128]{3,2,1,0:T(8,128)(2,1)}, bf16[3,16,16,128]{3,2,1,0:T(8,128)(2,1)S(1)}, u32[]{:S(2)}, u32[]{:S(2)}) collective-permute-start(bf16[3,16,16,128]{3,2,1,0:T(8,128)(2,1)} %get-tuple-element.21), channel_id=1, source_target_pairs={{1,2},{3,4},{5,6},{7,8},{9,10},{11,12},{13,14},{2,1},{4,3},{6,5},{... | collective-permute-start | bytes 589832 | tf_op jit(solution)/shard_map/ppermute | solution.py:466
  13.2 5.0 %collective-permute-start.1 = (bf16[3,16,16,128]{3,2,1,0:T(8,128)(2,1)}, bf16[3,16,16,128]{3,2,1,0:T(8,128)(2,1)S(1)}, u32[]{:S(2)}, u32[]{:S(2)}) collective-permute-start(bf16[3,16,16,128]{3,2,1,0:T(8,128)(2,1)} %get-tuple-element.22), channel_id=1, source_target_pairs={{0,1},{1,0},{2,3},{3,2},{4,5},{5,4},{6,7},{7,6},{8,9},{9,8},{10,11... | collective-permute-start | bytes 589832 | tf_op jit(solution)/shard_map/ppermute | solution.py:467
  13.4 1.6 %copy-start = (bf16[2,2,2,512,256]{4,3,2,1,0:T(8,128)(2,1)S(1)}, bf16[2,2,2,512,256]{4,3,2,1,0:T(8,128)(2,1)}, u32[]{:S(2)}) copy-start(bf16[2,2,2,512,256]{4,3,2,1,0:T(8,128)(2,1)} %param.14) | copy-start | bytes 6291460
  15.0 1.3 %copy-start.7 = (bf16[4,16,16,128]{3,2,1,0:T(8,128)(2,1)S(1)}, bf16[4,16,16,128]{3,2,1,0:T(8,128)(2,1)}, u32[]{:S(2)}) copy-start(bf16[4,16,16,128]{3,2,1,0:T(8,128)(2,1)} %volume.3) | copy-start | bytes 786436
  16.4 1.9 %copy-start.1 = (bf16[3,3,3,128,256]{4,3,2,1,0:T(8,128)(2,1)S(1)}, bf16[3,3,3,128,256]{4,3,2,1,0:T(8,128)(2,1)}, u32[]{:S(2)}) copy-start(bf16[3,3,3,128,256]{4,3,2,1,0:T(8,128)(2,1)} %param.11) | copy-start | bytes 5308420
  16.4 1.9 %copy-start.8 = (bf16[256,256]{1,0:T(8,128)(2,1)S(1)}, bf16[256,256]{1,0:T(8,128)(2,1)}, u32[]{:S(2)}) copy-start(bf16[256,256]{1,0:T(8,128)(2,1)} %constant.44.clone.order) | copy-start | bytes 393220
  18.3 17.6 %copy-start.5 = (bf16[3,3,3,256,32]{3,4,2,1,0:T(8,128)(2,1)S(1)}, bf16[3,3,3,256,32]{3,4,2,1,0:T(8,128)(2,1)}, u32[]{:S(2)}) copy-start(bf16[3,3,3,256,32]{3,4,2,1,0:T(8,128)(2,1)} %param.12) | copy-start | bytes 1327108
  21.1 31.9 %copy-start.3 = (bf16[3,3,3,512,32]{3,4,2,1,0:T(8,128)(2,1)S(1)}, bf16[3,3,3,512,32]{3,4,2,1,0:T(8,128)(2,1)}, u32[]{:S(2)}) copy-start(bf16[3,3,3,512,32]{3,4,2,1,0:T(8,128)(2,1)} %param.13) | copy-start | bytes 2654212
  21.2 5.4 %collective-permute-start.4 = (bf16[16,256]{1,0:T(8,128)(2,1)S(1)}, bf16[16,256]{1,0:T(8,128)(2,1)S(1)}, u32[]{:S(2)}, u32[]{:S(2)}) collective-permute-start(bf16[16,256]{1,0:T(8,128)(2,1)S(1)} %bitcast.33), channel_id=1, source_target_pairs={{0,12},{4,8},{8,4},{12,0},{1,13},{5,9},{9,5},{13,1},{2,14},{6,10},... | collective-permute-start | bytes 24584 | tf_op jit(solution)/shard_map/ppermute | solution.py:421
  25.2 4.1 %collective-permute-start.3 = (bf16[16,256]{1,0:T(8,128)(2,1)S(1)}, bf16[16,256]{1,0:T(8,128)(2,1)S(1)}, u32[]{:S(2)}, u32[]{:S(2)}) collective-permute-start(bf16[16,256]{1,0:T(8,128)(2,1)S(1)} %bitcast.34), channel_id=1, source_target_pairs={{0,8},{4,12},{8,0},{12,4},{1,9},{5,13},{9,1},{13,5},{2,10},{6,14},... | collective-permute-start | bytes 24584 | tf_op jit(solution)/shard_map/ppermute | solution.py:421
  25.2 4.1 %collective-permute-start.2 = (bf16[16,256]{1,0:T(8,128)(2,1)S(1)}, bf16[16,256]{1,0:T(8,128)(2,1)S(1)}, u32[]{:S(2)}, u32[]{:S(2)}) collective-permute-start(bf16[16,256]{1,0:T(8,128)(2,1)S(1)} %bitcast.35), channel_id=1, source_target_pairs={{0,4},{4,0},{8,12},{12,8},{1,5},{5,1},{9,13},{13,9},{2,6},{6,2},{1... | collective-permute-start | bytes 24584 | tf_op jit(solution)/shard_map/ppermute | solution.py:421
  29.9 2.2 %collective-permute-start.5 = (bf16[112,256]{1,0:T(8,128)(2,1)S(1)}, bf16[112,256]{1,0:T(8,128)(2,1)S(1)}, u32[]{:S(2)}, u32[]{:S(2)}) collective-permute-start(bf16[112,256]{1,0:T(8,128)(2,1)S(1)} %get-tuple-element.29), channel_id=1, source_target_pairs={{0,1},{1,0},{2,3},{3,2},{4,5},{5,4},{6,7},{7,6},{8,9},{9,8},{10,11... | collective-permute-start | bytes 172040 | tf_op jit(solution)/shard_map/ppermute | solution.py:421
  30.4 3.6 %collective-permute-start.6 = (bf16[112,256]{1,0:T(8,128)(2,1)S(1)}, bf16[112,256]{1,0:T(8,128)(2,1)S(1)}, u32[]{:S(2)}, u32[]{:S(2)}) collective-permute-start(bf16[112,256]{1,0:T(8,128)(2,1)S(1)} %get-tuple-element.30), channel_id=1, source_target_pairs={{0,2},{1,3},{2,0},{3,1},{4,6},{5,7},{6,4},{7,5},{8,10},{9,11},{10,... | collective-permute-start | bytes 172040 | tf_op jit(solution)/shard_map/ppermute | solution.py:421
  31.6 4.3 %collective-permute-start.7 = (bf16[112,256]{1,0:T(8,128)(2,1)S(1)}, bf16[112,256]{1,0:T(8,128)(2,1)S(1)}, u32[]{:S(2)}, u32[]{:S(2)}) collective-permute-start(bf16[112,256]{1,0:T(8,128)(2,1)S(1)} %get-tuple-element.31), channel_id=1, source_target_pairs={{0,3},{1,2},{2,1},{3,0},{4,7},{5,6},{6,5},{7,4},{8,11},{9,10},{10,... | collective-permute-start | bytes 172040 | tf_op jit(solution)/shard_map/ppermute | solution.py:421
  39.0 14.0 %all-to-all-start = ((bf16[16,32,256]{2,1,0:T(8,128)(2,1)}), bf16[16,32,256]{2,1,0:T(8,128)(2,1)S(1)}, u32[]{:S(2)}, u32[]{:S(2)}) async-start(bf16[16,32,256]{2,1,0:T(8,128)(2,1)} %shard_map.96), calls=%async_computation | async-start | bytes 524288 | tf_op jit(solution)/shard_map/all_to_all | solution.py:416
  44.3 20.4 %copy-start.6 = (bf16[2112,256]{1,0:T(8,128)(2,1)S(1)}, bf16[2112,256]{1,0:T(8,128)(2,1)}, u32[]{:S(2)}) copy-start(bf16[2112,256]{1,0:T(8,128)(2,1)} %all-gather.3.cloned.1.call-done) | copy-start | bytes 3244036
  46.5 18.1 %collective-permute-start.8 = (bf16[4,336,256]{2,1,0:T(8,128)(2,1)}, bf16[4,336,256]{2,1,0:T(8,128)(2,1)}, u32[]{:S(2)}, u32[]{:S(2)}) collective-permute-start(bf16[4,336,256]{2,1,0:T(8,128)(2,1)} %constant_dynamic-slice_fusion), channel_id=1, source_target_pairs={{0,16},{16,0},{1,17},{17,1},{2,18},{18,2},{3,19},{19,3},{4,20},{20... | collective-permute-start | bytes 2064392 | tf_op jit(solution)/shard_map/ppermute | solution.py:545
  54.3 19.7 %copy-start.4 = (bf16[2,2,2,256,128]{4,3,2,1,0:T(8,128)(2,1)S(1)}, bf16[2,2,2,256,128]{4,3,2,1,0:T(8,128)(2,1)}, u32[]{:S(2)}) copy-start(bf16[2,2,2,256,128]{4,3,2,1,0:T(8,128)(2,1)} %param.16) | copy-start | bytes 1572868
  67.5 2.9 %collective-permute-start.9 = (bf16[128,256]{1,0:T(8,128)(2,1)S(1)}, bf16[128,256]{1,0:T(8,128)(2,1)S(1)}, u32[]{:S(2)}, u32[]{:S(2)}) collective-permute-start(bf16[128,256]{1,0:T(8,128)(2,1)S(1)} %get-tuple-element.34), channel_id=1, source_target_pairs={{0,1},{1,0},{2,3},{3,2},{4,5},{5,4},{6,7},{7,6},{8,9},{9,8},{10,11... | collective-permute-start | bytes 196616 | tf_op jit(solution)/shard_map/ppermute | solution.py:421
  68.8 3.7 %collective-permute-start.10 = (bf16[128,256]{1,0:T(8,128)(2,1)S(1)}, bf16[128,256]{1,0:T(8,128)(2,1)S(1)}, u32[]{:S(2)}, u32[]{:S(2)}) collective-permute-start(bf16[128,256]{1,0:T(8,128)(2,1)S(1)} %get-tuple-element.35), channel_id=1, source_target_pairs={{0,2},{1,3},{2,0},{3,1},{4,6},{5,7},{6,4},{7,5},{8,10},{9,11},{10,... | collective-permute-start | bytes 196616 | tf_op jit(solution)/shard_map/ppermute | solution.py:421
  69.0 5.0 %collective-permute-start.11 = (bf16[128,256]{1,0:T(8,128)(2,1)S(1)}, bf16[128,256]{1,0:T(8,128)(2,1)S(1)}, u32[]{:S(2)}, u32[]{:S(2)}) collective-permute-start(bf16[128,256]{1,0:T(8,128)(2,1)S(1)} %get-tuple-element.36), channel_id=1, source_target_pairs={{0,3},{1,2},{2,1},{3,0},{4,7},{5,6},{6,5},{7,4},{8,11},{9,10},{10,... | collective-permute-start | bytes 196616 | tf_op jit(solution)/shard_map/ppermute | solution.py:421
Sparse Core Ops, SparseCore 0:
  8.9 31.1 all-gather.2
where the time goes:
time: 82.5 us; the launch traced here: 81.9 us
  starting transfers between devices  19.9 us (24%)
  waiting for transfers between devices  16.9 us (20%)
  Pallas kernels  15.3 us (19%)
  between operations  14.3 us (17%)
  blocking collectives  10.3 us (12%)
  local copies, waits for them, and re-layouts  5.21 us (6%)
    pallas_call x8, Pallas kernels, call(): pl.pallas_call(kernel, out_shape=outs, in_specs=[pl.BlockSpec(memory_spac...  13.2 us
    ppermute x9, waiting for transfers between devices, by_xor(): lax.ppermute(blocks[k], axis, swaps[k])  11.1 us
    all_to_all x1, blocking collectives, exchange(): lax.all_to_all(payload, axis, split_axis=0, concat_axis=0, tiled=True)  10.3 us
    ppermute x9, starting transfers between devices, by_xor(): lax.ppermute(blocks[k], axis, swaps[k])  9.56 us
    all_to_all x1, waiting for transfers between devices, exchange(): lax.all_to_all(payload, axis, split_axis=0, concat_axis=0, tiled=True)  5.33 us
    ppermute x1, starting transfers between devices, body(): off_chip = lax.ppermute(off_chip, ALL, pairs + [(j, i) for i, j in pairs])  4.54 us
    all_to_all x1, starting transfers between devices, exchange(): lax.all_to_all(payload, axis, split_axis=0, concat_axis=0, tiled=True)  4.52 us
    dynamic_slice x1, local copies, waits for them, and re-layouts, body(): piece = lax.dynamic_slice_in_dim(line, first_row, 336, axis=1)  2.22 us
  transfers between devices with their start and end apart: 14, of which 8 were waited for; matrix products, arithmetic and copies ran while one was open for 4% of the time, Pallas kernels for 11%

commit v1 on v0

--- a/solution.py
+++ b/solution.py
@@ -250,7 +250,8 @@
 
 
 def deep_stage(marks, weights, *refs):
-    near, out, parts = refs[:-2], refs[-2], refs[-1]
+    near, (out, after, parts) = refs[:-3], refs[-3:]
+    after[0] = 0
     _, chans, voxels = out.shape
     values = near[0][...] if len(near) == 1 else by_depth(marks, near, parts, 16)
     deep = spread_taps(weights, values, ((1,), (1,)), chans, voxels).astype(jnp.bfloat16)
@@ -526,22 +527,27 @@
         near = by_xor(skips, "r")
     blocks = pltpu.VMEM((GROUP, 48, 256), jnp.bfloat16)
 
-    deep = call(
+    deep, after = pl.pallas_call(
         deep_stage,
-        bf16((n, chans, voxels)),
-        [pltpu.VMEM((GROUP, 64, 256), jnp.bfloat16)],
-        (
-            marks,
-            deep_kernel.transpose(0, 1, 2, 4, 3).reshape(27 * chans, 256),
-            *pooled_whole,
+        out_shape=(bf16((n, chans, voxels)), jax.ShapeDtypeStruct((1,), jnp.int32)),
+        in_specs=[pl.BlockSpec(memory_space=pltpu.SMEM)]
+        + [pl.BlockSpec(memory_space=pltpu.VMEM)] * (1 + len(pooled_whole)),
+        out_specs=(
+            pl.BlockSpec(memory_space=pltpu.VMEM),
+            pl.BlockSpec(memory_space=pltpu.SMEM),
         ),
-        2 * 27 * chans * 256 * voxels,
-        16,
-        scalars=1,
+        scratch_shapes=[pltpu.VMEM((GROUP, 64, 256), jnp.bfloat16)],
+        compiler_params=pltpu.CompilerParams(vmem_limit_bytes=16 * MIB),
+        cost_estimate=pl.CostEstimate(
+            flops=2 * 27 * chans * 256 * voxels, bytes_accessed=10**6, transcendentals=0
+        ),
+    )(
+        marks,
+        deep_kernel.transpose(0, 1, 2, 4, 3).reshape(27 * chans, 256),
+        *pooled_whole,
     )
     if shared:
-        first_row = (deep[0, 0, 0] < 0).astype(jnp.int32)
-        piece = lax.dynamic_slice_in_dim(line, first_row, 336, axis=1)
+        piece = lax.dynamic_slice_in_dim(line, after[0], 336, axis=1)
         weights = (line, lax.ppermute(piece, "rep", [(0, 1), (1, 0)]))
     elif chans % 16:
         weights = line.reshape(planes, 27, chans, 256).transpose(1, 0, 2, 3)

time: 82.5 us -> 82.7 us (level)
  between operations: 14.3 us -> 15.6 us
  local copies, waits for them, and re-layouts: 5.21 us -> 3.94 us
    pallas_call x0 -> x1, Pallas kernels: none -> 1.85 us  [body(): pl.pallas_call(deep_stage, out_shape=(bf16((n, chans, voxels)), jax.Shape...]
    pallas_call x8 -> x7, Pallas kernels: 13.2 us -> 11.4 us  [call(): pl.pallas_call(kernel, out_shape=outs, in_specs=[pl.BlockSpec(memory_spac...]
    slice x1 -> x0, local copies, waits for them, and re-layouts: 1.27 us -> none  [body(): first_row = (deep[0, 0, 0] < 0).astype(jnp.int32)]
  transfers between devices with their start and end apart: 14 -> 14, of which waited for: 8 -> 8; matrix products, arithmetic and copies ran while one was open for 4% -> 3% of each run, Pallas kernels for 11% -> 11%
where the time goes in v1:
time: 82.7 us; the launch traced here: 82.1 us
  starting transfers between devices  19.9 us (24%)
  waiting for transfers between devices  16.9 us (20%)
  between operations  15.6 us (19%)
  Pallas kernels  15.3 us (19%)
  blocking collectives  10.3 us (12%)
  local copies, waits for them, and re-layouts  3.94 us (5%)
    pallas_call x7, Pallas kernels, call(): pl.pallas_call(kernel, out_shape=outs, in_specs=[pl.BlockSpec(memory_spac...  11.4 us
    ppermute x9, waiting for transfers between devices, by_xor(): lax.ppermute(blocks[k], axis, swaps[k])  11.1 us
    all_to_all x1, blocking collectives, exchange(): lax.all_to_all(payload, axis, split_axis=0, concat_axis=0, tiled=True)  10.3 us
    ppermute x9, starting transfers between devices, by_xor(): lax.ppermute(blocks[k], axis, swaps[k])  9.55 us
    all_to_all x1, waiting for transfers between devices, exchange(): lax.all_to_all(payload, axis, split_axis=0, concat_axis=0, tiled=True)  5.33 us
    ppermute x1, starting transfers between devices, body(): off_chip = lax.ppermute(off_chip, ALL, pairs + [(j, i) for i, j in pairs])  4.54 us
    all_to_all x1, starting transfers between devices, exchange(): lax.all_to_all(payload, axis, split_axis=0, concat_axis=0, tiled=True)  4.52 us
    dynamic_slice x1, local copies, waits for them, and re-layouts, body(): piece = lax.dynamic_slice_in_dim(line, after[0], 336, axis=1)  2.22 us
  transfers between devices with their start and end apart: 14, of which 8 were waited for; matrix products, arithmetic and copies ran while one was open for 3% of the time, Pallas kernels for 11%

profile of v1, /device:TPU:1, one launch (start us, length us, event | category | flops | bytes accessed | tf_op | source)
XLA Modules:
  0.0 82.1 jit_solution(635579810534905648)
XLA Ops:
  6.5 2.1 %shard_map.91 = (bf16[3,16,16,128]{3,2,1,0:T(8,128)(2,1)}, bf16[3,16,16,128]{3,2,1,0:T(8,128)(2,1)}, bf16[528,256]{1,0:T(8,128)(2,1)}) custom-call(s32[1]{0:T(128)} %bitcast.4.odd, s32[1]{0:T(128)} %bitcast.1.rep, bf16[4,16,16,128]{3,2,1,0:T(8,128)(2,1)} %volume.3, bf16[864,256]{1,0:T(8,128)(2,1)} %bitcast.37), custom_call_target="tpu_custom_call" | custom-call | bytes 1000000 | tf_op jit(solution)/shard_map/pallas_call | solution.py:452
  8.7 4.5 %collective-permute-start = (bf16[3,16,16,128]{3,2,1,0:T(8,128)(2,1)}, bf16[3,16,16,128]{3,2,1,0:T(8,128)(2,1)S(1)}, u32[]{:S(2)}, u32[]{:S(2)}) collective-permute-start(bf16[3,16,16,128]{3,2,1,0:T(8,128)(2,1)} %get-tuple-element.23), channel_id=1, source_target_pairs={{1,2},{3,4},{5,6},{7,8},{9,10},{11,12},{13,14},{2,1},{4,3},{6,5},{... | collective-permute-start | bytes 589832 | tf_op jit(solution)/shard_map/ppermute | solution.py:467
  13.3 0.1 stack.31.marks_ref.marks
  13.4 1.6 %copy-done = bf16[2,2,2,512,256]{4,3,2,1,0:T(8,128)(2,1)S(1)} copy-done((bf16[2,2,2,512,256]{4,3,2,1,0:T(8,128)(2,1)S(1)}, bf16[2,2,2,512,256]{4,3,2,1,0:T(8,128)(2,1)}, u32[]{:S(2)}) %copy-start) | copy-done | bytes 2097176
  15.0 1.3 %shard_map.93._.rise = bf16[512,512]{1,0:T(8,128)(2,1)S(1)} custom-call(s32[7]{0:T(128)S(1)} %stack.31.marks_ref.marks, bf16[8,512,256]{2,1,0:T(8,128)(2,1)S(1)} %bitcast.23), custom_call_target="tpu_custom_call" | custom-call | flops 134217728 | bytes 2097180 | tf_op jit(solution)/shard_map/pallas_call | solution.py:18
  16.4 1.4 %shard_map.92.own = f32[4,256,256]{2,1,0:T(8,128)S(1)} custom-call(bf16[4,16,16,128]{3,2,1,0:T(8,128)(2,1)S(1)} %copy-done.7, bf16[3,1152,128]{2,1,0:T(8,128)(2,1)S(1)} %bitcast.26), custom_call_target="tpu_custom_call" | custom-call | flops 1207959552 | bytes 1146880 | tf_op jit(solution)/shard_map/pallas_call | solution.py:18
  17.8 0.4 collective-permute-done.off_chip
  18.3 2.9 %shard_map.94 = (bf16[1,16,256]{2,1,0:T(8,128)(2,1)S(1)}, bf16[48,256]{1,0:T(8,128)(2,1)S(1)}, bf16[48,256]{1,0:T(8,128)(2,1)S(1)}, bf16[48,256]{1,0:T(8,128)(2,1)S(1)}, bf16[48,256]{1,0:T(8,128)(2,1)S(1)}) custom-call(s32[7]{0:T(128)S(1)} %stack.31.marks_ref.marks, bf16[3,16,16,128]{3,2,1,0:T(8,128)(2,1)S(1)} %collective-permute-done.off_chip, ...), custom_call_target="tpu_custom_call" | custom-call | flops 1207959552 | bytes 4227100 | tf_op jit(solution)/shard_map/pallas_call | solution.py:18
  21.1 4.0 %collective-permute-start.4 = (bf16[16,256]{1,0:T(8,128)(2,1)S(1)}, bf16[16,256]{1,0:T(8,128)(2,1)S(1)}, u32[]{:S(2)}, u32[]{:S(2)}) collective-permute-start(bf16[16,256]{1,0:T(8,128)(2,1)S(1)} %bitcast.33), channel_id=1, source_target_pairs={{0,12},{4,8},{8,4},{12,0},{1,13},{5,9},{9,5},{13,1},{2,14},{6,10},... | collective-permute-start | bytes 24584 | tf_op jit(solution)/shard_map/ppermute | solution.py:422
  25.2 0.4 collective-permute-start.2
  25.5 1.0 %collective-permute-done.4.refs_3_ = bf16[16,256]{1,0:T(8,128)(2,1)S(1)} collective-permute-done((bf16[16,256]{1,0:T(8,128)(2,1)S(1)}, bf16[16,256]{1,0:T(8,128)(2,1)S(1)}, u32[]{:S(2)}, u32[]{:S(2)}) %collective-permute-start.4) | collective-permute-done | bytes 8224 | tf_op jit(solution)/shard_map/ppermute | solution.py:422
  26.5 2.8 %collective-permute-done.3.refs_2_ = bf16[16,256]{1,0:T(8,128)(2,1)S(1)} collective-permute-done((bf16[16,256]{1,0:T(8,128)(2,1)S(1)}, bf16[16,256]{1,0:T(8,128)(2,1)S(1)}, u32[]{:S(2)}, u32[]{:S(2)}) %collective-permute-start.3) | collective-permute-done | bytes 8224 | tf_op jit(solution)/shard_map/ppermute | solution.py:422
  29.3 0.6 shard_map.95
  29.9 0.5 collective-permute-start.5
  30.4 1.3 %collective-permute-start.6 = (bf16[112,256]{1,0:T(8,128)(2,1)S(1)}, bf16[112,256]{1,0:T(8,128)(2,1)S(1)}, u32[]{:S(2)}, u32[]{:S(2)}) collective-permute-start(bf16[112,256]{1,0:T(8,128)(2,1)S(1)} %get-tuple-element.32), channel_id=1, source_target_pairs={{0,2},{1,3},{2,0},{3,1},{4,6},{5,7},{6,4},{7,5},{8,10},{9,11},{10,... | collective-permute-start | bytes 172040 | tf_op jit(solution)/shard_map/ppermute | solution.py:422
  31.6 0.5 collective-permute-start.7
  32.1 1.9 %collective-permute-done.6.refs_2_ = bf16[112,256]{1,0:T(8,128)(2,1)S(1)} collective-permute-done((bf16[112,256]{1,0:T(8,128)(2,1)S(1)}, bf16[112,256]{1,0:T(8,128)(2,1)S(1)}, u32[]{:S(2)}, u32[]{:S(2)}) %collective-permute-start.6) | collective-permute-done | bytes 57376 | tf_op jit(solution)/shard_map/ppermute | solution.py:422
  34.0 1.9 %collective-permute-done.7.refs_3_ = bf16[112,256]{1,0:T(8,128)(2,1)S(1)} collective-permute-done((bf16[112,256]{1,0:T(8,128)(2,1)S(1)}, bf16[112,256]{1,0:T(8,128)(2,1)S(1)}, u32[]{:S(2)}, u32[]{:S(2)}) %collective-permute-start.7) | collective-permute-done | bytes 57376 | tf_op jit(solution)/shard_map/ppermute | solution.py:422
  35.9 1.9 %shard_map.96 = (bf16[16,32,256]{2,1,0:T(8,128)(2,1)}, s32[1]{0:T(128)}) custom-call(s32[7]{0:T(128)S(1)} %stack.31.marks_ref.marks, bf16[864,256]{1,0:T(8,128)(2,1)S(1)} %bitcast.30, bf16[112,256]{1,0:T(8,128)(2,1)S(1)} %get-tuple-element.30.refs_0_, bf16[112,256]{1,0:T(8,128)(2,1)S(1)} %collective-permute-done.5.refs_1_, ...), custom_call_target="tpu_custom_call" | custom-call | flops 113246208 | bytes 1000000 | tf_op jit(solution)/shard_map/pallas_call | solution.py:530
  39.1 4.5 %all-to-all-start = ((bf16[16,32,256]{2,1,0:T(8,128)(2,1)}), bf16[16,32,256]{2,1,0:T(8,128)(2,1)S(1)}, u32[]{:S(2)}, u32[]{:S(2)}) async-start(bf16[16,32,256]{2,1,0:T(8,128)(2,1)} %get-tuple-element.34), calls=%async_computation | async-start | bytes 524288 | tf_op jit(solution)/shard_map/all_to_all | solution.py:417
  44.4 2.2 %constant_dynamic-slice_fusion = bf16[4,336,256]{2,1,0:T(8,128)(2,1)} fusion(bf16[4,528,256]{2,1,0:T(8,128)(2,1)} %bitcast.31, s32[]{:T(128)S(6)} %select_n.18), kind=kLoop, calls=%fused_computation | loop fusion | bytes 1376260 | tf_op jit(solution)/shard_map/dynamic_slice | solution.py:550
  46.6 1.2 %collective-permute-start.8 = (bf16[4,336,256]{2,1,0:T(8,128)(2,1)}, bf16[4,336,256]{2,1,0:T(8,128)(2,1)}, u32[]{:S(2)}, u32[]{:S(2)}) collective-permute-start(bf16[4,336,256]{2,1,0:T(8,128)(2,1)} %constant_dynamic-slice_fusion), channel_id=1, source_target_pairs={{0,16},{16,0},{1,17},{17,1},{2,18},{18,2},{3,19},{19,3},{4,20},{20... | collective-permute-start | bytes 2064392 | tf_op jit(solution)/shard_map/ppermute | solution.py:551
  47.8 5.3 %all-to-all-done = bf16[16,32,256]{2,1,0:T(8,128)(2,1)S(1)} async-done(((bf16[16,32,256]{2,1,0:T(8,128)(2,1)}), bf16[16,32,256]{2,1,0:T(8,128)(2,1)S(1)}, u32[]{:S(2)}, u32[]{:S(2)}) %all-to-all-start) | async-done | bytes 262176 | tf_op jit(solution)/shard_map/all_to_all | solution.py:417
  53.2 1.3 %shard_map.97 = bf16[16,32,128]{2,1,0:T(8,128)(2,1)S(1)} custom-call(s32[7]{0:T(128)S(1)} %stack.31.marks_ref.marks, bf16[864,512]{1,0:T(8,128)(2,1)S(1)} %bitcast.28, bf16[112,256]{1,0:T(8,128)(2,1)S(1)} %get-tuple-element.30.refs_0_, bf16[112,256]{1,0:T(8,128)(2,1)S(1)} %collective-permute-done.5.refs_1_, ...), custom_call_target="tpu_custom_call" | custom-call | flops 226492416 | bytes 1376284 | tf_op jit(solution)/shard_map/pallas_call | solution.py:18
  54.4 10.3 %all_to_all.10.deeper = bf16[16,32,128]{2,1,0:T(8,128)(2,1)S(1)} all-to-all(bf16[16,32,128]{2,1,0:T(8,128)(2,1)S(1)} %shard_map.97), channel_id=1, replica_groups=mesh['rep'=2,'z'=4,'r'=4] {'z','r'}, dimensions={0} | all-to-all | bytes 262144 | tf_op jit(solution)/shard_map/all_to_all | solution.py:417
  64.8 2.9 %shard_map.98 = (bf16[128,256]{1,0:T(8,128)(2,1)S(1)}, bf16[128,256]{1,0:T(8,128)(2,1)S(1)}, bf16[128,256]{1,0:T(8,128)(2,1)S(1)}, bf16[128,256]{1,0:T(8,128)(2,1)S(1)}) custom-call(s32[7]{0:T(128)S(1)} %stack.31.marks_ref.marks, bf16[16,32,128]{2,1,0:T(8,128)(2,1)S(1)} %all_to_all.10.deeper, bf16[512,512]{1,0:T(8,128)(2,1)S(1)} %shard_map.93._.rise, ...), custom_call_target="tpu_custom_call" | custom-call | flops 905969664 | bytes 2654236 | tf_op jit(solution)/shard_map/pallas_call | solution.py:18
  67.7 1.2 %collective-permute-start.9 = (bf16[128,256]{1,0:T(8,128)(2,1)S(1)}, bf16[128,256]{1,0:T(8,128)(2,1)S(1)}, u32[]{:S(2)}, u32[]{:S(2)}) collective-permute-start(bf16[128,256]{1,0:T(8,128)(2,1)S(1)} %get-tuple-element.38), channel_id=1, source_target_pairs={{0,1},{1,0},{2,3},{3,2},{4,5},{5,4},{6,7},{7,6},{8,9},{9,8},{10,11... | collective-permute-start | bytes 196616 | tf_op jit(solution)/shard_map/ppermute | solution.py:422
  68.9 0.2 collective-permute-start.10
  69.2 1.5 %collective-permute-start.11 = (bf16[128,256]{1,0:T(8,128)(2,1)S(1)}, bf16[128,256]{1,0:T(8,128)(2,1)S(1)}, u32[]{:S(2)}, u32[]{:S(2)}) collective-permute-start(bf16[128,256]{1,0:T(8,128)(2,1)S(1)} %get-tuple-element.40), channel_id=1, source_target_pairs={{0,3},{1,2},{2,1},{3,0},{4,7},{5,6},{6,5},{7,4},{8,11},{9,10},{10,... | collective-permute-start | bytes 196616 | tf_op jit(solution)/shard_map/ppermute | solution.py:422
  70.6 2.0 %collective-permute-done.10.refs_2_ = bf16[128,256]{1,0:T(8,128)(2,1)S(1)} collective-permute-done((bf16[128,256]{1,0:T(8,128)(2,1)S(1)}, bf16[128,256]{1,0:T(8,128)(2,1)S(1)}, u32[]{:S(2)}, u32[]{:S(2)}) %collective-permute-start.10) | collective-permute-done | bytes 65568 | tf_op jit(solution)/shard_map/ppermute | solution.py:422
  72.6 1.6 %collective-permute-done.11.refs_3_ = bf16[128,256]{1,0:T(8,128)(2,1)S(1)} collective-permute-done((bf16[128,256]{1,0:T(8,128)(2,1)S(1)}, bf16[128,256]{1,0:T(8,128)(2,1)S(1)}, u32[]{:S(2)}, u32[]{:S(2)}) %collective-permute-start.11) | collective-permute-done | bytes 65568 | tf_op jit(solution)/shard_map/ppermute | solution.py:422
  74.1 1.1 %shard_map.99 = bf16[1024,128]{1,0:T(8,128)(2,1)} custom-call(bf16[128,256]{1,0:T(8,128)(2,1)S(1)} %get-tuple-element.37.refs_0_, bf16[128,256]{1,0:T(8,128)(2,1)S(1)} %collective-permute-done.9.refs_1_, bf16[128,256]{1,0:T(8,128)(2,1)S(1)} %collective-permute-done.10.refs_2_, bf16[128,256]{1,0:T(8,128)(2,1)S(1)} %collective-permute-done.11.refs_3_, ...), custom_call_target="tpu_custom_call" | custom-call | flops 67108864 | bytes 786432 | tf_op jit(solution)/shard_map/pallas_call | solution.py:18
  (27 shorter events, 0.2 us)
Async XLA Ops:
  6.5 37.8 %all-gather.3.cloned.1.call-start = ((), (), s32[]{:S(2)}) async-start(), calls=%async_computation.2 | async-start | bytes 1351680 | tf_op jit(solution)/shard_map/all_gather | solution.py:471
  6.5 9.8 %copy-start.2 = (bf16[3,3,3,128,128]{4,3,2,1,0:T(8,128)(2,1)S(1)}, bf16[3,3,3,128,128]{4,3,2,1,0:T(8,128)(2,1)}, u32[]{:S(2)}) copy-start(bf16[3,3,3,128,128]{4,3,2,1,0:T(8,128)(2,1)} %param.10) | copy-start | bytes 2654212
  8.7 9.6 %collective-permute-start = (bf16[3,16,16,128]{3,2,1,0:T(8,128)(2,1)}, bf16[3,16,16,128]{3,2,1,0:T(8,128)(2,1)S(1)}, u32[]{:S(2)}, u32[]{:S(2)}) collective-permute-start(bf16[3,16,16,128]{3,2,1,0:T(8,128)(2,1)} %get-tuple-element.23), channel_id=1, source_target_pairs={{1,2},{3,4},{5,6},{7,8},{9,10},{11,12},{13,14},{2,1},{4,3},{6,5},{... | collective-permute-start | bytes 589832 | tf_op jit(solution)/shard_map/ppermute | solution.py:467
  13.2 5.0 %collective-permute-start.1 = (bf16[3,16,16,128]{3,2,1,0:T(8,128)(2,1)}, bf16[3,16,16,128]{3,2,1,0:T(8,128)(2,1)S(1)}, u32[]{:S(2)}, u32[]{:S(2)}) collective-permute-start(bf16[3,16,16,128]{3,2,1,0:T(8,128)(2,1)} %get-tuple-element.24), channel_id=1, source_target_pairs={{0,1},{1,0},{2,3},{3,2},{4,5},{5,4},{6,7},{7,6},{8,9},{9,8},{10,11... | collective-permute-start | bytes 589832 | tf_op jit(solution)/shard_map/ppermute | solution.py:468
  13.4 1.6 %copy-start = (bf16[2,2,2,512,256]{4,3,2,1,0:T(8,128)(2,1)S(1)}, bf16[2,2,2,512,256]{4,3,2,1,0:T(8,128)(2,1)}, u32[]{:S(2)}) copy-start(bf16[2,2,2,512,256]{4,3,2,1,0:T(8,128)(2,1)} %param.14) | copy-start | bytes 6291460
  15.0 1.3 %copy-start.7 = (bf16[4,16,16,128]{3,2,1,0:T(8,128)(2,1)S(1)}, bf16[4,16,16,128]{3,2,1,0:T(8,128)(2,1)}, u32[]{:S(2)}) copy-start(bf16[4,16,16,128]{3,2,1,0:T(8,128)(2,1)} %volume.3) | copy-start | bytes 786436
  16.4 1.9 %copy-start.1 = (bf16[3,3,3,128,256]{4,3,2,1,0:T(8,128)(2,1)S(1)}, bf16[3,3,3,128,256]{4,3,2,1,0:T(8,128)(2,1)}, u32[]{:S(2)}) copy-start(bf16[3,3,3,128,256]{4,3,2,1,0:T(8,128)(2,1)} %param.11) | copy-start | bytes 5308420
  16.4 1.9 %copy-start.8 = (bf16[256,256]{1,0:T(8,128)(2,1)S(1)}, bf16[256,256]{1,0:T(8,128)(2,1)}, u32[]{:S(2)}) copy-start(bf16[256,256]{1,0:T(8,128)(2,1)} %constant.41.clone.order) | copy-start | bytes 393220
  18.2 17.6 %copy-start.5 = (bf16[3,3,3,256,32]{3,4,2,1,0:T(8,128)(2,1)S(1)}, bf16[3,3,3,256,32]{3,4,2,1,0:T(8,128)(2,1)}, u32[]{:S(2)}) copy-start(bf16[3,3,3,256,32]{3,4,2,1,0:T(8,128)(2,1)} %param.12) | copy-start | bytes 1327108
  21.1 32.0 %copy-start.3 = (bf16[3,3,3,512,32]{3,4,2,1,0:T(8,128)(2,1)S(1)}, bf16[3,3,3,512,32]{3,4,2,1,0:T(8,128)(2,1)}, u32[]{:S(2)}) copy-start(bf16[3,3,3,512,32]{3,4,2,1,0:T(8,128)(2,1)} %param.13) | copy-start | bytes 2654212
  21.1 5.4 %collective-permute-start.4 = (bf16[16,256]{1,0:T(8,128)(2,1)S(1)}, bf16[16,256]{1,0:T(8,128)(2,1)S(1)}, u32[]{:S(2)}, u32[]{:S(2)}) collective-permute-start(bf16[16,256]{1,0:T(8,128)(2,1)S(1)} %bitcast.33), channel_id=1, source_target_pairs={{0,12},{4,8},{8,4},{12,0},{1,13},{5,9},{9,5},{13,1},{2,14},{6,10},... | collective-permute-start | bytes 24584 | tf_op jit(solution)/shard_map/ppermute | solution.py:422
  25.2 4.1 %collective-permute-start.3 = (bf16[16,256]{1,0:T(8,128)(2,1)S(1)}, bf16[16,256]{1,0:T(8,128)(2,1)S(1)}, u32[]{:S(2)}, u32[]{:S(2)}) collective-permute-start(bf16[16,256]{1,0:T(8,128)(2,1)S(1)} %bitcast.34), channel_id=1, source_target_pairs={{0,8},{4,12},{8,0},{12,4},{1,9},{5,13},{9,1},{13,5},{2,10},{6,14},... | collective-permute-start | bytes 24584 | tf_op jit(solution)/shard_map/ppermute | solution.py:422
  25.2 4.1 %collective-permute-start.2 = (bf16[16,256]{1,0:T(8,128)(2,1)S(1)}, bf16[16,256]{1,0:T(8,128)(2,1)S(1)}, u32[]{:S(2)}, u32[]{:S(2)}) collective-permute-start(bf16[16,256]{1,0:T(8,128)(2,1)S(1)} %bitcast.35), channel_id=1, source_target_pairs={{0,4},{4,0},{8,12},{12,8},{1,5},{5,1},{9,13},{13,9},{2,6},{6,2},{1... | collective-permute-start | bytes 24584 | tf_op jit(solution)/shard_map/ppermute | solution.py:422
  29.9 2.2 %collective-permute-start.5 = (bf16[112,256]{1,0:T(8,128)(2,1)S(1)}, bf16[112,256]{1,0:T(8,128)(2,1)S(1)}, u32[]{:S(2)}, u32[]{:S(2)}) collective-permute-start(bf16[112,256]{1,0:T(8,128)(2,1)S(1)} %get-tuple-element.31), channel_id=1, source_target_pairs={{0,1},{1,0},{2,3},{3,2},{4,5},{5,4},{6,7},{7,6},{8,9},{9,8},{10,11... | collective-permute-start | bytes 172040 | tf_op jit(solution)/shard_map/ppermute | solution.py:422
  30.4 3.6 %collective-permute-start.6 = (bf16[112,256]{1,0:T(8,128)(2,1)S(1)}, bf16[112,256]{1,0:T(8,128)(2,1)S(1)}, u32[]{:S(2)}, u32[]{:S(2)}) collective-permute-start(bf16[112,256]{1,0:T(8,128)(2,1)S(1)} %get-tuple-element.32), channel_id=1, source_target_pairs={{0,2},{1,3},{2,0},{3,1},{4,6},{5,7},{6,4},{7,5},{8,10},{9,11},{10,... | collective-permute-start | bytes 172040 | tf_op jit(solution)/shard_map/ppermute | solution.py:422
  31.6 4.3 %collective-permute-start.7 = (bf16[112,256]{1,0:T(8,128)(2,1)S(1)}, bf16[112,256]{1,0:T(8,128)(2,1)S(1)}, u32[]{:S(2)}, u32[]{:S(2)}) collective-permute-start(bf16[112,256]{1,0:T(8,128)(2,1)S(1)} %get-tuple-element.33), channel_id=1, source_target_pairs={{0,3},{1,2},{2,1},{3,0},{4,7},{5,6},{6,5},{7,4},{8,11},{9,10},{10,... | collective-permute-start | bytes 172040 | tf_op jit(solution)/shard_map/ppermute | solution.py:422
  39.1 14.0 %all-to-all-start = ((bf16[16,32,256]{2,1,0:T(8,128)(2,1)}), bf16[16,32,256]{2,1,0:T(8,128)(2,1)S(1)}, u32[]{:S(2)}, u32[]{:S(2)}) async-start(bf16[16,32,256]{2,1,0:T(8,128)(2,1)} %get-tuple-element.34), calls=%async_computation | async-start | bytes 524288 | tf_op jit(solution)/shard_map/all_to_all | solution.py:417
  44.4 20.4 %copy-start.6 = (bf16[2112,256]{1,0:T(8,128)(2,1)S(1)}, bf16[2112,256]{1,0:T(8,128)(2,1)}, u32[]{:S(2)}) copy-start(bf16[2112,256]{1,0:T(8,128)(2,1)} %all-gather.3.cloned.1.call-done) | copy-start | bytes 3244036
  46.6 18.2 %collective-permute-start.8 = (bf16[4,336,256]{2,1,0:T(8,128)(2,1)}, bf16[4,336,256]{2,1,0:T(8,128)(2,1)}, u32[]{:S(2)}, u32[]{:S(2)}) collective-permute-start(bf16[4,336,256]{2,1,0:T(8,128)(2,1)} %constant_dynamic-slice_fusion), channel_id=1, source_target_pairs={{0,16},{16,0},{1,17},{17,1},{2,18},{18,2},{3,19},{19,3},{4,20},{20... | collective-permute-start | bytes 2064392 | tf_op jit(solution)/shard_map/ppermute | solution.py:551
  54.4 19.7 %copy-start.4 = (bf16[2,2,2,256,128]{4,3,2,1,0:T(8,128)(2,1)S(1)}, bf16[2,2,2,256,128]{4,3,2,1,0:T(8,128)(2,1)}, u32[]{:S(2)}) copy-start(bf16[2,2,2,256,128]{4,3,2,1,0:T(8,128)(2,1)} %param.16) | copy-start | bytes 1572868
  67.7 2.9 %collective-permute-start.9 = (bf16[128,256]{1,0:T(8,128)(2,1)S(1)}, bf16[128,256]{1,0:T(8,128)(2,1)S(1)}, u32[]{:S(2)}, u32[]{:S(2)}) collective-permute-start(bf16[128,256]{1,0:T(8,128)(2,1)S(1)} %get-tuple-element.38), channel_id=1, source_target_pairs={{0,1},{1,0},{2,3},{3,2},{4,5},{5,4},{6,7},{7,6},{8,9},{9,8},{10,11... | collective-permute-start | bytes 196616 | tf_op jit(solution)/shard_map/ppermute | solution.py:422
  68.9 3.7 %collective-permute-start.10 = (bf16[128,256]{1,0:T(8,128)(2,1)S(1)}, bf16[128,256]{1,0:T(8,128)(2,1)S(1)}, u32[]{:S(2)}, u32[]{:S(2)}) collective-permute-start(bf16[128,256]{1,0:T(8,128)(2,1)S(1)} %get-tuple-element.39), channel_id=1, source_target_pairs={{0,2},{1,3},{2,0},{3,1},{4,6},{5,7},{6,4},{7,5},{8,10},{9,11},{10,... | collective-permute-start | bytes 196616 | tf_op jit(solution)/shard_map/ppermute | solution.py:422
  69.2 5.0 %collective-permute-start.11 = (bf16[128,256]{1,0:T(8,128)(2,1)S(1)}, bf16[128,256]{1,0:T(8,128)(2,1)S(1)}, u32[]{:S(2)}, u32[]{:S(2)}) collective-permute-start(bf16[128,256]{1,0:T(8,128)(2,1)S(1)} %get-tuple-element.40), channel_id=1, source_target_pairs={{0,3},{1,2},{2,1},{3,0},{4,7},{5,6},{6,5},{7,4},{8,11},{9,10},{10,... | collective-permute-start | bytes 196616 | tf_op jit(solution)/shard_map/ppermute | solution.py:422
Sparse Core Ops, SparseCore 0:
  8.9 31.1 all-gather.2

commit v2 on v0

--- a/solution.py
+++ b/solution.py
@@ -97,6 +97,12 @@
         copy.start()
     for copy in copies:
         copy.wait()
+
+
+def pick_stage(line, _, out, done):
+    copy = pltpu.make_async_copy(line.at[:, pl.ds(0, out.shape[1])], out, done)
+    copy.start()
+    copy.wait()
 
 
 def own_stage(volume, weights, out, shifted):
@@ -540,8 +546,15 @@
         scalars=1,
     )
     if shared:
-        first_row = (deep[0, 0, 0] < 0).astype(jnp.int32)
-        piece = lax.dynamic_slice_in_dim(line, first_row, 336, axis=1)
+        piece = call(
+            pick_stage,
+            bf16((planes, 336, 256)),
+            [pltpu.SemaphoreType.DMA],
+            (line, deep),
+            0,
+            16,
+            unread=2,
+        )
         weights = (line, lax.ppermute(piece, "rep", [(0, 1), (1, 0)]))
     elif chans % 16:
         weights = line.reshape(planes, 27, chans, 256).transpose(1, 0, 2, 3)

time: 82.5 us -> 84.9 us (1.029)
  waiting for transfers between devices: 16.9 us -> 18.4 us
  local copies, waits for them, and re-layouts: 5.21 us -> 6.48 us
    unnamed x18 -> x38, local copies, waits for them, and re-layouts: 1.63 us -> 6.39 us
    dynamic_slice x1 -> x0, local copies, waits for them, and re-layouts: 2.22 us -> none  [body(): piece = lax.dynamic_slice_in_dim(line, first_row, 336, axis=1)]
    all_to_all x1, waiting for transfers between devices: 5.33 us -> 6.85 us  [exchange(): lax.all_to_all(payload, axis, split_axis=0, concat_axis=0, tiled=True)]
    slice x1 -> x0, local copies, waits for them, and re-layouts: 1.27 us -> none  [body(): first_row = (deep[0, 0, 0] < 0).astype(jnp.int32)]
    pallas_call x8 -> x9, Pallas kernels: 13.2 us -> 13.3 us  [call(): pl.pallas_call(kernel, out_shape=outs, in_specs=[pl.BlockSpec(memory_spac...]
  transfers between devices with their start and end apart: 14 -> 14, of which waited for: 8 -> 8; matrix products, arithmetic and copies ran while one was open for 4% -> 0% of each run, Pallas kernels for 11% -> 11%
where the time goes in v2:
time: 84.9 us; the launch traced here: 84.2 us
  starting transfers between devices  20 us (24%)
  waiting for transfers between devices  18.4 us (22%)
  Pallas kernels  15.4 us (18%)
  between operations  13.6 us (16%)
  blocking collectives  10.3 us (12%)
  local copies, waits for them, and re-layouts  6.48 us (8%)
    pallas_call x9, Pallas kernels, call(): pl.pallas_call(kernel, out_shape=outs, in_specs=[pl.BlockSpec(memory_spac...  13.3 us
    ppermute x9, waiting for transfers between devices, by_xor(): lax.ppermute(blocks[k], axis, swaps[k])  11.1 us
    all_to_all x1, blocking collectives, exchange(): lax.all_to_all(payload, axis, split_axis=0, concat_axis=0, tiled=True)  10.3 us
    ppermute x9, starting transfers between devices, by_xor(): lax.ppermute(blocks[k], axis, swaps[k])  9.56 us
    all_to_all x1, waiting for transfers between devices, exchange(): lax.all_to_all(payload, axis, split_axis=0, concat_axis=0, tiled=True)  6.85 us
    unnamed x38, local copies, waits for them, and re-layouts  6.39 us
    ppermute x1, starting transfers between devices, body(): off_chip = lax.ppermute(off_chip, ALL, pairs + [(j, i) for i, j in pairs])  4.54 us
    all_to_all x1, starting transfers between devices, exchange(): lax.all_to_all(payload, axis, split_axis=0, concat_axis=0, tiled=True)  4.52 us
  transfers between devices with their start and end apart: 14, of which 8 were waited for; matrix products, arithmetic and copies ran while one was open for 0% of the time, Pallas kernels for 11%

profile of v2, /device:TPU:1, one launch (start us, length us, event | category | flops | bytes accessed | tf_op | source)
XLA Modules:
  0.0 84.2 jit_solution(10873755934126865093)
XLA Ops:
  6.5 2.1 %shard_map.91 = (bf16[3,16,16,128]{3,2,1,0:T(8,128)(2,1)}, bf16[3,16,16,128]{3,2,1,0:T(8,128)(2,1)}, bf16[528,256]{1,0:T(8,128)(2,1)}) custom-call(s32[1]{0:T(128)} %bitcast.4.odd, s32[1]{0:T(128)} %bitcast.1.rep, bf16[4,16,16,128]{3,2,1,0:T(8,128)(2,1)} %volume.3, bf16[864,256]{1,0:T(8,128)(2,1)} %bitcast.36), custom_call_target="tpu_custom_call" | custom-call | bytes 1000000 | tf_op jit(solution)/shard_map/pallas_call | solution.py:457
  8.7 4.5 %collective-permute-start = (bf16[3,16,16,128]{3,2,1,0:T(8,128)(2,1)}, bf16[3,16,16,128]{3,2,1,0:T(8,128)(2,1)S(1)}, u32[]{:S(2)}, u32[]{:S(2)}) collective-permute-start(bf16[3,16,16,128]{3,2,1,0:T(8,128)(2,1)} %get-tuple-element.21), channel_id=1, source_target_pairs={{1,2},{3,4},{5,6},{7,8},{9,10},{11,12},{13,14},{2,1},{4,3},{6,5},{... | collective-permute-start | bytes 589832 | tf_op jit(solution)/shard_map/ppermute | solution.py:472
  13.4 1.6 %copy-done = bf16[2,2,2,512,256]{4,3,2,1,0:T(8,128)(2,1)S(1)} copy-done((bf16[2,2,2,512,256]{4,3,2,1,0:T(8,128)(2,1)S(1)}, bf16[2,2,2,512,256]{4,3,2,1,0:T(8,128)(2,1)}, u32[]{:S(2)}) %copy-start) | copy-done | bytes 2097176
  15.0 1.3 %shard_map.93._.rise = bf16[512,512]{1,0:T(8,128)(2,1)S(1)} custom-call(s32[7]{0:T(128)S(1)} %stack.31.marks_ref.marks, bf16[8,512,256]{2,1,0:T(8,128)(2,1)S(1)} %bitcast.22), custom_call_target="tpu_custom_call" | custom-call | flops 134217728 | bytes 2097180 | tf_op jit(solution)/shard_map/pallas_call | solution.py:18
  16.4 1.4 %shard_map.92.own = f32[4,256,256]{2,1,0:T(8,128)S(1)} custom-call(bf16[4,16,16,128]{3,2,1,0:T(8,128)(2,1)S(1)} %copy-done.8, bf16[3,1152,128]{2,1,0:T(8,128)(2,1)S(1)} %bitcast.27), custom_call_target="tpu_custom_call" | custom-call | flops 1207959552 | bytes 1146880 | tf_op jit(solution)/shard_map/pallas_call | solution.py:18
  18.3 2.9 %shard_map.94 = (bf16[1,16,256]{2,1,0:T(8,128)(2,1)S(1)}, bf16[48,256]{1,0:T(8,128)(2,1)S(1)}, bf16[48,256]{1,0:T(8,128)(2,1)S(1)}, bf16[48,256]{1,0:T(8,128)(2,1)S(1)}, bf16[48,256]{1,0:T(8,128)(2,1)S(1)}) custom-call(s32[7]{0:T(128)S(1)} %stack.31.marks_ref.marks, bf16[3,16,16,128]{3,2,1,0:T(8,128)(2,1)S(1)} %collective-permute-done.off_chip, ...), custom_call_target="tpu_custom_call" | custom-call | flops 1207959552 | bytes 4227100 | tf_op jit(solution)/shard_map/pallas_call | solution.py:18
  21.1 4.0 %collective-permute-start.4 = (bf16[16,256]{1,0:T(8,128)(2,1)S(1)}, bf16[16,256]{1,0:T(8,128)(2,1)S(1)}, u32[]{:S(2)}, u32[]{:S(2)}) collective-permute-start(bf16[16,256]{1,0:T(8,128)(2,1)S(1)} %bitcast.32), channel_id=1, source_target_pairs={{0,12},{4,8},{8,4},{12,0},{1,13},{5,9},{9,5},{13,1},{2,14},{6,10},... | collective-permute-start | bytes 24584 | tf_op jit(solution)/shard_map/ppermute | solution.py:427
  25.5 1.0 %collective-permute-done.4.refs_3_ = bf16[16,256]{1,0:T(8,128)(2,1)S(1)} collective-permute-done((bf16[16,256]{1,0:T(8,128)(2,1)S(1)}, bf16[16,256]{1,0:T(8,128)(2,1)S(1)}, u32[]{:S(2)}, u32[]{:S(2)}) %collective-permute-start.4) | collective-permute-done | bytes 8224 | tf_op jit(solution)/shard_map/ppermute | solution.py:427
  26.5 2.8 %collective-permute-done.3.refs_2_ = bf16[16,256]{1,0:T(8,128)(2,1)S(1)} collective-permute-done((bf16[16,256]{1,0:T(8,128)(2,1)S(1)}, bf16[16,256]{1,0:T(8,128)(2,1)S(1)}, u32[]{:S(2)}, u32[]{:S(2)}) %collective-permute-start.3) | collective-permute-done | bytes 8224 | tf_op jit(solution)/shard_map/ppermute | solution.py:427
  29.3 0.6 shard_map.95
  29.9 0.5 collective-permute-start.5
  30.4 1.3 %collective-permute-start.6 = (bf16[112,256]{1,0:T(8,128)(2,1)S(1)}, bf16[112,256]{1,0:T(8,128)(2,1)S(1)}, u32[]{:S(2)}, u32[]{:S(2)}) collective-permute-start(bf16[112,256]{1,0:T(8,128)(2,1)S(1)} %get-tuple-element.30), channel_id=1, source_target_pairs={{0,2},{1,3},{2,0},{3,1},{4,6},{5,7},{6,4},{7,5},{8,10},{9,11},{10,... | collective-permute-start | bytes 172040 | tf_op jit(solution)/shard_map/ppermute | solution.py:427
  32.1 1.9 %collective-permute-done.6.refs_2_ = bf16[112,256]{1,0:T(8,128)(2,1)S(1)} collective-permute-done((bf16[112,256]{1,0:T(8,128)(2,1)S(1)}, bf16[112,256]{1,0:T(8,128)(2,1)S(1)}, u32[]{:S(2)}, u32[]{:S(2)}) %collective-permute-start.6) | collective-permute-done | bytes 57376 | tf_op jit(solution)/shard_map/ppermute | solution.py:427
  34.0 1.9 %collective-permute-done.7.refs_3_ = bf16[112,256]{1,0:T(8,128)(2,1)S(1)} collective-permute-done((bf16[112,256]{1,0:T(8,128)(2,1)S(1)}, bf16[112,256]{1,0:T(8,128)(2,1)S(1)}, u32[]{:S(2)}, u32[]{:S(2)}) %collective-permute-start.7) | collective-permute-done | bytes 57376 | tf_op jit(solution)/shard_map/ppermute | solution.py:427
  35.9 1.8 %shard_map.96._ = bf16[16,32,256]{2,1,0:T(8,128)(2,1)} custom-call(s32[7]{0:T(128)S(1)} %stack.31.marks_ref.marks, bf16[864,256]{1,0:T(8,128)(2,1)S(1)} %bitcast.31, bf16[112,256]{1,0:T(8,128)(2,1)S(1)} %get-tuple-element.28.refs_0_, bf16[112,256]{1,0:T(8,128)(2,1)S(1)} %collective-permute-done.5.refs_1_, ...), custom_call_target="tpu_custom_call" | custom-call | flops 113246208 | bytes 671772 | tf_op jit(solution)/shard_map/pallas_call | solution.py:18
  37.8 0.6 copy-done.9
  38.4 0.6 copy-done.12
  39.0 4.5 %all-to-all-start = ((bf16[16,32,256]{2,1,0:T(8,128)(2,1)}), bf16[16,32,256]{2,1,0:T(8,128)(2,1)S(1)}, u32[]{:S(2)}, u32[]{:S(2)}) async-start(bf16[16,32,256]{2,1,0:T(8,128)(2,1)} %shard_map.96._), calls=%async_computation | async-start | bytes 524288 | tf_op jit(solution)/shard_map/all_to_all | solution.py:422
  43.5 1.2 %copy-done.2 = bf16[2112,256]{1,0:T(8,128)(2,1)S(1)} copy-done((bf16[2112,256]{1,0:T(8,128)(2,1)S(1)}, bf16[2112,256]{1,0:T(8,128)(2,1)}, u32[]{:S(2)}) %copy-start.2) | copy-done | bytes 1081368
  44.9 1.3 %collective-permute-start.8 = (bf16[4,336,256]{2,1,0:T(8,128)(2,1)S(1)}, bf16[4,336,256]{2,1,0:T(8,128)(2,1)}, u32[]{:S(2)}, u32[]{:S(2)}) collective-permute-start(bf16[4,336,256]{2,1,0:T(8,128)(2,1)S(1)} %shard_map.98), channel_id=1, source_target_pairs={{0,16},{16,0},{1,17},{17,1},{2,18},{18,2},{3,19},{19,3},{4,20},{20... | collective-permute-start | bytes 2064392 | tf_op jit(solution)/shard_map/ppermute | solution.py:558
  46.2 6.8 %all-to-all-done = bf16[16,32,256]{2,1,0:T(8,128)(2,1)S(1)} async-done(((bf16[16,32,256]{2,1,0:T(8,128)(2,1)}), bf16[16,32,256]{2,1,0:T(8,128)(2,1)S(1)}, u32[]{:S(2)}, u32[]{:S(2)}) %all-to-all-start) | async-done | bytes 262176 | tf_op jit(solution)/shard_map/all_to_all | solution.py:422
  53.0 0.8 copy-done.10
  53.8 0.8 copy-done.13
  54.7 0.6 copy-done.17
  55.3 1.3 %shard_map.97 = bf16[16,32,128]{2,1,0:T(8,128)(2,1)S(1)} custom-call(s32[7]{0:T(128)S(1)} %copy-done.17, bf16[864,512]{1,0:T(8,128)(2,1)S(1)} %bitcast.29, bf16[112,256]{1,0:T(8,128)(2,1)S(1)} %get-tuple-element.28.refs_0_, bf16[112,256]{1,0:T(8,128)(2,1)S(1)} %collective-permute-done.5.refs_1_, bf16[112,256]{1,0:T(8,128)(2,1)S(1)} %copy-done.10, ...), custom_call_target="tpu_custom_call" | custom-call | flops 226492416 | bytes 1376284 | tf_op jit(solution)/shard_map/pallas_call | solution.py:18
  56.6 10.3 %all_to_all.10.deeper = bf16[16,32,128]{2,1,0:T(8,128)(2,1)S(1)} all-to-all(bf16[16,32,128]{2,1,0:T(8,128)(2,1)S(1)} %shard_map.97), channel_id=1, replica_groups=mesh['rep'=2,'z'=4,'r'=4] {'z','r'}, dimensions={0} | all-to-all | bytes 262144 | tf_op jit(solution)/shard_map/all_to_all | solution.py:422
  66.9 2.9 %shard_map.99 = (bf16[128,256]{1,0:T(8,128)(2,1)S(1)}, bf16[128,256]{1,0:T(8,128)(2,1)S(1)}, bf16[128,256]{1,0:T(8,128)(2,1)S(1)}, bf16[128,256]{1,0:T(8,128)(2,1)S(1)}) custom-call(s32[7]{0:T(128)S(1)} %copy-done.18, bf16[16,32,128]{2,1,0:T(8,128)(2,1)S(1)} %all_to_all.10.deeper, bf16[512,512]{1,0:T(8,128)(2,1)S(1)} %shard_map.93._.rise, ...), custom_call_target="tpu_custom_call" | custom-call | flops 905969664 | bytes 2654236 | tf_op jit(solution)/shard_map/pallas_call | solution.py:18
  69.8 1.2 %collective-permute-start.9 = (bf16[128,256]{1,0:T(8,128)(2,1)S(1)}, bf16[128,256]{1,0:T(8,128)(2,1)S(1)}, u32[]{:S(2)}, u32[]{:S(2)}) collective-permute-start(bf16[128,256]{1,0:T(8,128)(2,1)S(1)} %get-tuple-element.34), channel_id=1, source_target_pairs={{0,1},{1,0},{2,3},{3,2},{4,5},{5,4},{6,7},{7,6},{8,9},{9,8},{10,11... | collective-permute-start | bytes 196616 | tf_op jit(solution)/shard_map/ppermute | solution.py:427
  71.1 1.7 %collective-permute-start.11 = (bf16[128,256]{1,0:T(8,128)(2,1)S(1)}, bf16[128,256]{1,0:T(8,128)(2,1)S(1)}, u32[]{:S(2)}, u32[]{:S(2)}) collective-permute-start(bf16[128,256]{1,0:T(8,128)(2,1)S(1)} %get-tuple-element.36), channel_id=1, source_target_pairs={{0,3},{1,2},{2,1},{3,0},{4,7},{5,6},{6,5},{7,4},{8,11},{9,10},{10,... | collective-permute-start | bytes 196616 | tf_op jit(solution)/shard_map/ppermute | solution.py:427
  72.8 2.0 %collective-permute-done.10.refs_2_ = bf16[128,256]{1,0:T(8,128)(2,1)S(1)} collective-permute-done((bf16[128,256]{1,0:T(8,128)(2,1)S(1)}, bf16[128,256]{1,0:T(8,128)(2,1)S(1)}, u32[]{:S(2)}, u32[]{:S(2)}) %collective-permute-start.10) | collective-permute-done | bytes 65568 | tf_op jit(solution)/shard_map/ppermute | solution.py:427
  74.8 1.6 %collective-permute-done.11.refs_3_ = bf16[128,256]{1,0:T(8,128)(2,1)S(1)} collective-permute-done((bf16[128,256]{1,0:T(8,128)(2,1)S(1)}, bf16[128,256]{1,0:T(8,128)(2,1)S(1)}, u32[]{:S(2)}, u32[]{:S(2)}) %collective-permute-start.11) | collective-permute-done | bytes 65568 | tf_op jit(solution)/shard_map/ppermute | solution.py:427
  76.3 1.1 %shard_map.100 = bf16[1024,128]{1,0:T(8,128)(2,1)} custom-call(bf16[128,256]{1,0:T(8,128)(2,1)S(1)} %get-tuple-element.33.refs_0_, bf16[128,256]{1,0:T(8,128)(2,1)S(1)} %collective-permute-done.9.refs_1_, bf16[128,256]{1,0:T(8,128)(2,1)S(1)} %collective-permute-done.10.refs_2_, bf16[128,256]{1,0:T(8,128)(2,1)S(1)} %collective-permute-done.11.refs_3_, ...), custom_call_target="tpu_custom_call" | custom-call | flops 67108864 | bytes 786432 | tf_op jit(solution)/shard_map/pallas_call | solution.py:18
  (47 shorter events, 1.6 us)
Async XLA Ops:
  6.5 37.0 %all-gather.3.cloned.1.call-start = ((), (), s32[]{:S(2)}) async-start(), calls=%async_computation.2 | async-start | bytes 1351680 | tf_op jit(solution)/shard_map/all_gather | solution.py:476
  6.5 9.8 %copy-start.4 = (bf16[3,3,3,128,128]{4,3,2,1,0:T(8,128)(2,1)S(1)}, bf16[3,3,3,128,128]{4,3,2,1,0:T(8,128)(2,1)}, u32[]{:S(2)}) copy-start(bf16[3,3,3,128,128]{4,3,2,1,0:T(8,128)(2,1)} %param.10) | copy-start | bytes 2654212
  8.7 9.6 %collective-permute-start = (bf16[3,16,16,128]{3,2,1,0:T(8,128)(2,1)}, bf16[3,16,16,128]{3,2,1,0:T(8,128)(2,1)S(1)}, u32[]{:S(2)}, u32[]{:S(2)}) collective-permute-start(bf16[3,16,16,128]{3,2,1,0:T(8,128)(2,1)} %get-tuple-element.21), channel_id=1, source_target_pairs={{1,2},{3,4},{5,6},{7,8},{9,10},{11,12},{13,14},{2,1},{4,3},{6,5},{... | collective-permute-start | bytes 589832 | tf_op jit(solution)/shard_map/ppermute | solution.py:472
  13.2 5.0 %collective-permute-start.1 = (bf16[3,16,16,128]{3,2,1,0:T(8,128)(2,1)}, bf16[3,16,16,128]{3,2,1,0:T(8,128)(2,1)S(1)}, u32[]{:S(2)}, u32[]{:S(2)}) collective-permute-start(bf16[3,16,16,128]{3,2,1,0:T(8,128)(2,1)} %get-tuple-element.22), channel_id=1, source_target_pairs={{0,1},{1,0},{2,3},{3,2},{4,5},{5,4},{6,7},{7,6},{8,9},{9,8},{10,11... | collective-permute-start | bytes 589832 | tf_op jit(solution)/shard_map/ppermute | solution.py:473
  13.4 22.5 %copy-start.16 = (s32[7]{0:T(128)}, s32[7]{0:T(128)S(1)}, u32[]{:S(2)}) copy-start(s32[7]{0:T(128)S(1)} %stack.31.marks_ref.marks) | copy-start | bytes 88
  13.4 1.6 %copy-start = (bf16[2,2,2,512,256]{4,3,2,1,0:T(8,128)(2,1)S(1)}, bf16[2,2,2,512,256]{4,3,2,1,0:T(8,128)(2,1)}, u32[]{:S(2)}) copy-start(bf16[2,2,2,512,256]{4,3,2,1,0:T(8,128)(2,1)} %param.14) | copy-start | bytes 6291460
  15.0 1.3 %copy-start.8 = (bf16[4,16,16,128]{3,2,1,0:T(8,128)(2,1)S(1)}, bf16[4,16,16,128]{3,2,1,0:T(8,128)(2,1)}, u32[]{:S(2)}) copy-start(bf16[4,16,16,128]{3,2,1,0:T(8,128)(2,1)} %volume.3) | copy-start | bytes 786436
  16.4 1.9 %copy-start.1 = (bf16[3,3,3,128,256]{4,3,2,1,0:T(8,128)(2,1)S(1)}, bf16[3,3,3,128,256]{4,3,2,1,0:T(8,128)(2,1)}, u32[]{:S(2)}) copy-start(bf16[3,3,3,128,256]{4,3,2,1,0:T(8,128)(2,1)} %param.11) | copy-start | bytes 5308420
  16.4 1.9 %copy-start.15 = (bf16[256,256]{1,0:T(8,128)(2,1)S(1)}, bf16[256,256]{1,0:T(8,128)(2,1)}, u32[]{:S(2)}) copy-start(bf16[256,256]{1,0:T(8,128)(2,1)} %constant.38.clone.order) | copy-start | bytes 393220
  18.3 17.7 %copy-start.7 = (bf16[3,3,3,256,32]{3,4,2,1,0:T(8,128)(2,1)S(1)}, bf16[3,3,3,256,32]{3,4,2,1,0:T(8,128)(2,1)}, u32[]{:S(2)}) copy-start(bf16[3,3,3,256,32]{3,4,2,1,0:T(8,128)(2,1)} %param.12) | copy-start | bytes 1327108
  21.1 5.4 %collective-permute-start.4 = (bf16[16,256]{1,0:T(8,128)(2,1)S(1)}, bf16[16,256]{1,0:T(8,128)(2,1)S(1)}, u32[]{:S(2)}, u32[]{:S(2)}) collective-permute-start(bf16[16,256]{1,0:T(8,128)(2,1)S(1)} %bitcast.32), channel_id=1, source_target_pairs={{0,12},{4,8},{8,4},{12,0},{1,13},{5,9},{9,5},{13,1},{2,14},{6,10},... | collective-permute-start | bytes 24584 | tf_op jit(solution)/shard_map/ppermute | solution.py:427
  25.2 4.1 %collective-permute-start.3 = (bf16[16,256]{1,0:T(8,128)(2,1)S(1)}, bf16[16,256]{1,0:T(8,128)(2,1)S(1)}, u32[]{:S(2)}, u32[]{:S(2)}) collective-permute-start(bf16[16,256]{1,0:T(8,128)(2,1)S(1)} %bitcast.33), channel_id=1, source_target_pairs={{0,8},{4,12},{8,0},{12,4},{1,9},{5,13},{9,1},{13,5},{2,10},{6,14},... | collective-permute-start | bytes 24584 | tf_op jit(solution)/shard_map/ppermute | solution.py:427
  25.2 4.1 %collective-permute-start.2 = (bf16[16,256]{1,0:T(8,128)(2,1)S(1)}, bf16[16,256]{1,0:T(8,128)(2,1)S(1)}, u32[]{:S(2)}, u32[]{:S(2)}) collective-permute-start(bf16[16,256]{1,0:T(8,128)(2,1)S(1)} %bitcast.34), channel_id=1, source_target_pairs={{0,4},{4,0},{8,12},{12,8},{1,5},{5,1},{9,13},{13,9},{2,6},{6,2},{1... | collective-permute-start | bytes 24584 | tf_op jit(solution)/shard_map/ppermute | solution.py:427
  29.9 23.2 %copy-start.5 = (bf16[3,3,3,512,32]{3,4,2,1,0:T(8,128)(2,1)S(1)}, bf16[3,3,3,512,32]{3,4,2,1,0:T(8,128)(2,1)}, u32[]{:S(2)}) copy-start(bf16[3,3,3,512,32]{3,4,2,1,0:T(8,128)(2,1)} %param.13) | copy-start | bytes 2654212
  29.9 2.2 %collective-permute-start.5 = (bf16[112,256]{1,0:T(8,128)(2,1)S(1)}, bf16[112,256]{1,0:T(8,128)(2,1)S(1)}, u32[]{:S(2)}, u32[]{:S(2)}) collective-permute-start(bf16[112,256]{1,0:T(8,128)(2,1)S(1)} %get-tuple-element.29), channel_id=1, source_target_pairs={{0,1},{1,0},{2,3},{3,2},{4,5},{5,4},{6,7},{7,6},{8,9},{9,8},{10,11... | collective-permute-start | bytes 172040 | tf_op jit(solution)/shard_map/ppermute | solution.py:427
  30.4 3.6 %collective-permute-start.6 = (bf16[112,256]{1,0:T(8,128)(2,1)S(1)}, bf16[112,256]{1,0:T(8,128)(2,1)S(1)}, u32[]{:S(2)}, u32[]{:S(2)}) collective-permute-start(bf16[112,256]{1,0:T(8,128)(2,1)S(1)} %get-tuple-element.30), channel_id=1, source_target_pairs={{0,2},{1,3},{2,0},{3,1},{4,6},{5,7},{6,4},{7,5},{8,10},{9,11},{10,... | collective-permute-start | bytes 172040 | tf_op jit(solution)/shard_map/ppermute | solution.py:427
  31.6 4.3 %collective-permute-start.7 = (bf16[112,256]{1,0:T(8,128)(2,1)S(1)}, bf16[112,256]{1,0:T(8,128)(2,1)S(1)}, u32[]{:S(2)}, u32[]{:S(2)}) collective-permute-start(bf16[112,256]{1,0:T(8,128)(2,1)S(1)} %get-tuple-element.31), channel_id=1, source_target_pairs={{0,3},{1,2},{2,1},{3,0},{4,7},{5,6},{6,5},{7,4},{8,11},{9,10},{10,... | collective-permute-start | bytes 172040 | tf_op jit(solution)/shard_map/ppermute | solution.py:427
  37.8 0.6 copy-start.9
  39.0 14.0 %all-to-all-start = ((bf16[16,32,256]{2,1,0:T(8,128)(2,1)}), bf16[16,32,256]{2,1,0:T(8,128)(2,1)S(1)}, u32[]{:S(2)}, u32[]{:S(2)}) async-start(bf16[16,32,256]{2,1,0:T(8,128)(2,1)} %shard_map.96._), calls=%async_computation | async-start | bytes 524288 | tf_op jit(solution)/shard_map/all_to_all | solution.py:422
  43.5 1.2 %copy-start.2 = (bf16[2112,256]{1,0:T(8,128)(2,1)S(1)}, bf16[2112,256]{1,0:T(8,128)(2,1)}, u32[]{:S(2)}) copy-start(bf16[2112,256]{1,0:T(8,128)(2,1)} %all-gather.3.cloned.1.call-done) | copy-start | bytes 3244036
  44.8 22.1 %copy-start.3 = (bf16[2112,256]{1,0:T(8,128)(2,1)S(1)}, bf16[2112,256]{1,0:T(8,128)(2,1)}, u32[]{:S(2)}) copy-start(bf16[2112,256]{1,0:T(8,128)(2,1)} %all-gather.3.cloned.1.call-done) | copy-start | bytes 3244036
  44.9 22.0 %collective-permute-start.8 = (bf16[4,336,256]{2,1,0:T(8,128)(2,1)S(1)}, bf16[4,336,256]{2,1,0:T(8,128)(2,1)}, u32[]{:S(2)}, u32[]{:S(2)}) collective-permute-start(bf16[4,336,256]{2,1,0:T(8,128)(2,1)S(1)} %shard_map.98), channel_id=1, source_target_pairs={{0,16},{16,0},{1,17},{17,1},{2,18},{18,2},{3,19},{19,3},{4,20},{20... | collective-permute-start | bytes 2064392 | tf_op jit(solution)/shard_map/ppermute | solution.py:558
  53.0 13.9 %copy-start.18 = (s32[7]{0:T(128)S(1)}, s32[7]{0:T(128)}, u32[]{:S(2)}) copy-start(s32[7]{0:T(128)} %copy-done.16) | copy-start | bytes 88
  53.0 0.8 copy-start.10
  53.8 0.8 copy-start.13
  54.7 0.6 copy-start.17
  55.3 11.6 %copy-start.11 = (bf16[112,256]{1,0:T(8,128)(2,1)S(1)}, bf16[112,256]{1,0:T(8,128)(2,1)}, u32[]{:S(2)}) copy-start(bf16[112,256]{1,0:T(8,128)(2,1)} %copy-done.9) | copy-start | bytes 172036
  55.3 11.6 %copy-start.14 = (bf16[112,256]{1,0:T(8,128)(2,1)S(1)}, bf16[112,256]{1,0:T(8,128)(2,1)}, u32[]{:S(2)}) copy-start(bf16[112,256]{1,0:T(8,128)(2,1)} %copy-done.12) | copy-start | bytes 172036
  56.6 19.8 %copy-start.6 = (bf16[2,2,2,256,128]{4,3,2,1,0:T(8,128)(2,1)S(1)}, bf16[2,2,2,256,128]{4,3,2,1,0:T(8,128)(2,1)}, u32[]{:S(2)}) copy-start(bf16[2,2,2,256,128]{4,3,2,1,0:T(8,128)(2,1)} %param.16) | copy-start | bytes 1572868
  69.8 2.9 %collective-permute-start.9 = (bf16[128,256]{1,0:T(8,128)(2,1)S(1)}, bf16[128,256]{1,0:T(8,128)(2,1)S(1)}, u32[]{:S(2)}, u32[]{:S(2)}) collective-permute-start(bf16[128,256]{1,0:T(8,128)(2,1)S(1)} %get-tuple-element.34), channel_id=1, source_target_pairs={{0,1},{1,0},{2,3},{3,2},{4,5},{5,4},{6,7},{7,6},{8,9},{9,8},{10,11... | collective-permute-start | bytes 196616 | tf_op jit(solution)/shard_map/ppermute | solution.py:427
  71.1 3.7 %collective-permute-start.10 = (bf16[128,256]{1,0:T(8,128)(2,1)S(1)}, bf16[128,256]{1,0:T(8,128)(2,1)S(1)}, u32[]{:S(2)}, u32[]{:S(2)}) collective-permute-start(bf16[128,256]{1,0:T(8,128)(2,1)S(1)} %get-tuple-element.35), channel_id=1, source_target_pairs={{0,2},{1,3},{2,0},{3,1},{4,6},{5,7},{6,4},{7,5},{8,10},{9,11},{10,... | collective-permute-start | bytes 196616 | tf_op jit(solution)/shard_map/ppermute | solution.py:427
  71.1 5.2 %collective-permute-start.11 = (bf16[128,256]{1,0:T(8,128)(2,1)S(1)}, bf16[128,256]{1,0:T(8,128)(2,1)S(1)}, u32[]{:S(2)}, u32[]{:S(2)}) collective-permute-start(bf16[128,256]{1,0:T(8,128)(2,1)S(1)} %get-tuple-element.36), channel_id=1, source_target_pairs={{0,3},{1,2},{2,1},{3,0},{4,7},{5,6},{6,5},{7,4},{8,11},{9,10},{10,... | collective-permute-start | bytes 196616 | tf_op jit(solution)/shard_map/ppermute | solution.py:427
  (1 other events, 0.6 us)
Sparse Core Ops, SparseCore 0:
  8.9 31.1 all-gather.2

commit v3 on v0

--- a/solution.py
+++ b/solution.py
@@ -540,9 +540,7 @@
         scalars=1,
     )
     if shared:
-        first_row = (deep[0, 0, 0] < 0).astype(jnp.int32)
-        piece = lax.dynamic_slice_in_dim(line, first_row, 336, axis=1)
-        weights = (line, lax.ppermute(piece, "rep", [(0, 1), (1, 0)]))
+        weights = (line, lax.ppermute(line[:, :336], "rep", [(0, 1), (1, 0)]))
     elif chans % 16:
         weights = line.reshape(planes, 27, chans, 256).transpose(1, 0, 2, 3)
         weights = (weights.reshape(1, 27 * 128, 256),)

time: 82.5 us -> 80.6 us (0.977)
  local copies, waits for them, and re-layouts: 5.21 us -> 3.82 us
    dynamic_slice x1 -> x0, local copies, waits for them, and re-layouts: 2.22 us -> none  [body(): piece = lax.dynamic_slice_in_dim(line, first_row, 336, axis=1)]
    all_to_all x1, starting transfers between devices: 4.52 us -> 3.66 us  [exchange(): lax.all_to_all(payload, axis, split_axis=0, concat_axis=0, tiled=True)]
    slice x1, local copies, waits for them, and re-layouts: 1.27 us -> 2.09 us  [body(): weights = (line, lax.ppermute(line[:, :336], 'rep', [(0, 1), (1, 0)]))]
  transfers between devices with their start and end apart: 14 -> 14, of which waited for: 8 -> 8; matrix products, arithmetic and copies ran while one was open for 4% -> 3% of each run, Pallas kernels for 11% -> 12%
where the time goes in v3:
time: 80.6 us; the launch traced here: 80.2 us
  starting transfers between devices  19.7 us (24%)
  waiting for transfers between devices  17.5 us (22%)
  Pallas kernels  15.3 us (19%)
  between operations  13.6 us (17%)
  blocking collectives  10.3 us (13%)
  local copies, waits for them, and re-layouts  3.82 us (5%)
    pallas_call x8, Pallas kernels, call(): pl.pallas_call(kernel, out_shape=outs, in_specs=[pl.BlockSpec(memory_spac...  13.2 us
    ppermute x9, waiting for transfers between devices, by_xor(): lax.ppermute(blocks[k], axis, swaps[k])  10.9 us
    all_to_all x1, blocking collectives, exchange(): lax.all_to_all(payload, axis, split_axis=0, concat_axis=0, tiled=True)  10.3 us
    ppermute x9, starting transfers between devices, by_xor(): lax.ppermute(blocks[k], axis, swaps[k])  10.2 us
    all_to_all x1, waiting for transfers between devices, exchange(): lax.all_to_all(payload, axis, split_axis=0, concat_axis=0, tiled=True)  6.13 us
    ppermute x1, starting transfers between devices, body(): off_chip = lax.ppermute(off_chip, ALL, pairs + [(j, i) for i, j in pairs])  4.54 us
    all_to_all x1, starting transfers between devices, exchange(): lax.all_to_all(payload, axis, split_axis=0, concat_axis=0, tiled=True)  3.66 us
    pallas_call x1, Pallas kernels, body(): pl.pallas_call(front_stage, out_shape=(halo, halo) + (bf16((528, 256)),)...  2.11 us
  transfers between devices with their start and end apart: 14, of which 8 were waited for; matrix products, arithmetic and copies ran while one was open for 3% of the time, Pallas kernels for 12%

profile of v3, /device:TPU:1, one launch (start us, length us, event | category | flops | bytes accessed | tf_op | source)
XLA Modules:
  0.0 80.2 jit_solution(5567311034102882904)
XLA Ops:
  6.5 2.1 %shard_map.91 = (bf16[3,16,16,128]{3,2,1,0:T(8,128)(2,1)}, bf16[3,16,16,128]{3,2,1,0:T(8,128)(2,1)}, bf16[528,256]{1,0:T(8,128)(2,1)}) custom-call(s32[1]{0:T(128)} %bitcast.4.odd, s32[1]{0:T(128)} %bitcast.1.rep, bf16[4,16,16,128]{3,2,1,0:T(8,128)(2,1)} %volume.3, bf16[864,256]{1,0:T(8,128)(2,1)} %bitcast.36), custom_call_target="tpu_custom_call" | custom-call | bytes 1000000 | tf_op jit(solution)/shard_map/pallas_call | solution.py:451
  8.7 4.5 %collective-permute-start = (bf16[3,16,16,128]{3,2,1,0:T(8,128)(2,1)}, bf16[3,16,16,128]{3,2,1,0:T(8,128)(2,1)S(1)}, u32[]{:S(2)}, u32[]{:S(2)}) collective-permute-start(bf16[3,16,16,128]{3,2,1,0:T(8,128)(2,1)} %get-tuple-element.21), channel_id=1, source_target_pairs={{1,2},{3,4},{5,6},{7,8},{9,10},{11,12},{13,14},{2,1},{4,3},{6,5},{... | collective-permute-start | bytes 589832 | tf_op jit(solution)/shard_map/ppermute | solution.py:466
  13.2 0.1 collective-permute-start.1
  13.3 0.1 stack.31.marks_ref.marks
  13.4 1.6 %copy-done = bf16[2,2,2,512,256]{4,3,2,1,0:T(8,128)(2,1)S(1)} copy-done((bf16[2,2,2,512,256]{4,3,2,1,0:T(8,128)(2,1)S(1)}, bf16[2,2,2,512,256]{4,3,2,1,0:T(8,128)(2,1)}, u32[]{:S(2)}) %copy-start) | copy-done | bytes 2097176
  15.0 1.3 %shard_map.93._.rise = bf16[512,512]{1,0:T(8,128)(2,1)S(1)} custom-call(s32[7]{0:T(128)S(1)} %stack.31.marks_ref.marks, bf16[8,512,256]{2,1,0:T(8,128)(2,1)S(1)} %bitcast.22), custom_call_target="tpu_custom_call" | custom-call | flops 134217728 | bytes 2097180 | tf_op jit(solution)/shard_map/pallas_call | solution.py:18
  16.4 1.4 %shard_map.92.own = f32[4,256,256]{2,1,0:T(8,128)S(1)} custom-call(bf16[4,16,16,128]{3,2,1,0:T(8,128)(2,1)S(1)} %copy-done.7, bf16[3,1152,128]{2,1,0:T(8,128)(2,1)S(1)} %bitcast.25), custom_call_target="tpu_custom_call" | custom-call | flops 1207959552 | bytes 1146880 | tf_op jit(solution)/shard_map/pallas_call | solution.py:18
  17.8 0.4 collective-permute-done.off_chip
  18.3 2.9 %shard_map.94 = (bf16[1,16,256]{2,1,0:T(8,128)(2,1)S(1)}, bf16[48,256]{1,0:T(8,128)(2,1)S(1)}, bf16[48,256]{1,0:T(8,128)(2,1)S(1)}, bf16[48,256]{1,0:T(8,128)(2,1)S(1)}, bf16[48,256]{1,0:T(8,128)(2,1)S(1)}) custom-call(s32[7]{0:T(128)S(1)} %stack.31.marks_ref.marks, bf16[3,16,16,128]{3,2,1,0:T(8,128)(2,1)S(1)} %collective-permute-done.off_chip, ...), custom_call_target="tpu_custom_call" | custom-call | flops 1207959552 | bytes 4227100 | tf_op jit(solution)/shard_map/pallas_call | solution.py:18
  21.2 2.0 %collective-permute-start.2 = (bf16[16,256]{1,0:T(8,128)(2,1)S(1)}, bf16[16,256]{1,0:T(8,128)(2,1)S(1)}, u32[]{:S(2)}, u32[]{:S(2)}) collective-permute-start(bf16[16,256]{1,0:T(8,128)(2,1)S(1)} %bitcast.32), channel_id=1, source_target_pairs={{0,4},{4,0},{8,12},{12,8},{1,5},{5,1},{9,13},{13,9},{2,6},{6,2},{1... | collective-permute-start | bytes 24584 | tf_op jit(solution)/shard_map/ppermute | solution.py:421
  23.2 2.3 %collective-permute-start.3 = (bf16[16,256]{1,0:T(8,128)(2,1)S(1)}, bf16[16,256]{1,0:T(8,128)(2,1)S(1)}, u32[]{:S(2)}, u32[]{:S(2)}) collective-permute-start(bf16[16,256]{1,0:T(8,128)(2,1)S(1)} %bitcast.33), channel_id=1, source_target_pairs={{0,8},{4,12},{8,0},{12,4},{1,9},{5,13},{9,1},{13,5},{2,10},{6,14},... | collective-permute-start | bytes 24584 | tf_op jit(solution)/shard_map/ppermute | solution.py:421
  25.5 2.2 %collective-permute-done.3.refs_2_ = bf16[16,256]{1,0:T(8,128)(2,1)S(1)} collective-permute-done((bf16[16,256]{1,0:T(8,128)(2,1)S(1)}, bf16[16,256]{1,0:T(8,128)(2,1)S(1)}, u32[]{:S(2)}, u32[]{:S(2)}) %collective-permute-start.3) | collective-permute-done | bytes 8224 | tf_op jit(solution)/shard_map/ppermute | solution.py:421
  27.7 2.3 %collective-permute-done.4.refs_3_ = bf16[16,256]{1,0:T(8,128)(2,1)S(1)} collective-permute-done((bf16[16,256]{1,0:T(8,128)(2,1)S(1)}, bf16[16,256]{1,0:T(8,128)(2,1)S(1)}, u32[]{:S(2)}, u32[]{:S(2)}) %collective-permute-start.4) | collective-permute-done | bytes 8224 | tf_op jit(solution)/shard_map/ppermute | solution.py:421
  30.0 0.6 shard_map.95
  30.5 1.3 %collective-permute-start.5 = (bf16[112,256]{1,0:T(8,128)(2,1)S(1)}, bf16[112,256]{1,0:T(8,128)(2,1)S(1)}, u32[]{:S(2)}, u32[]{:S(2)}) collective-permute-start(bf16[112,256]{1,0:T(8,128)(2,1)S(1)} %get-tuple-element.29), channel_id=1, source_target_pairs={{0,1},{1,0},{2,3},{3,2},{4,5},{5,4},{6,7},{7,6},{8,9},{9,8},{10,11... | collective-permute-start | bytes 172040 | tf_op jit(solution)/shard_map/ppermute | solution.py:421
  31.8 0.8 %collective-permute-start.6 = (bf16[112,256]{1,0:T(8,128)(2,1)S(1)}, bf16[112,256]{1,0:T(8,128)(2,1)S(1)}, u32[]{:S(2)}, u32[]{:S(2)}) collective-permute-start(bf16[112,256]{1,0:T(8,128)(2,1)S(1)} %get-tuple-element.30), channel_id=1, source_target_pairs={{0,2},{1,3},{2,0},{3,1},{4,6},{5,7},{6,4},{7,5},{8,10},{9,11},{10,... | collective-permute-start | bytes 172040 | tf_op jit(solution)/shard_map/ppermute | solution.py:421
  32.6 0.9 %collective-permute-start.7 = (bf16[112,256]{1,0:T(8,128)(2,1)S(1)}, bf16[112,256]{1,0:T(8,128)(2,1)S(1)}, u32[]{:S(2)}, u32[]{:S(2)}) collective-permute-start(bf16[112,256]{1,0:T(8,128)(2,1)S(1)} %get-tuple-element.31), channel_id=1, source_target_pairs={{0,3},{1,2},{2,1},{3,0},{4,7},{5,6},{6,5},{7,4},{8,11},{9,10},{10,... | collective-permute-start | bytes 172040 | tf_op jit(solution)/shard_map/ppermute | solution.py:421
  33.5 1.9 %collective-permute-done.6.refs_2_ = bf16[112,256]{1,0:T(8,128)(2,1)S(1)} collective-permute-done((bf16[112,256]{1,0:T(8,128)(2,1)S(1)}, bf16[112,256]{1,0:T(8,128)(2,1)S(1)}, u32[]{:S(2)}, u32[]{:S(2)}) %collective-permute-start.6) | collective-permute-done | bytes 57376 | tf_op jit(solution)/shard_map/ppermute | solution.py:421
  35.4 1.7 %collective-permute-done.7.refs_3_ = bf16[112,256]{1,0:T(8,128)(2,1)S(1)} collective-permute-done((bf16[112,256]{1,0:T(8,128)(2,1)S(1)}, bf16[112,256]{1,0:T(8,128)(2,1)S(1)}, u32[]{:S(2)}, u32[]{:S(2)}) %collective-permute-start.7) | collective-permute-done | bytes 57376 | tf_op jit(solution)/shard_map/ppermute | solution.py:421
  37.1 1.8 %shard_map.96 = bf16[16,32,256]{2,1,0:T(8,128)(2,1)} custom-call(s32[7]{0:T(128)S(1)} %stack.31.marks_ref.marks, bf16[864,256]{1,0:T(8,128)(2,1)S(1)} %bitcast.29, bf16[112,256]{1,0:T(8,128)(2,1)S(1)} %get-tuple-element.28.refs_0_, bf16[112,256]{1,0:T(8,128)(2,1)S(1)} %collective-permute-done.5.refs_1_, bf16[112,256]{1,0:T(8,128)(2,1)S(1)} %collective-permute-done.6.refs_2_, ...), custom_call_target="tpu_custom_call" | custom-call | flops 113246208 | bytes 671772 | tf_op jit(solution)/shard_map/pallas_call | solution.py:18
  38.9 3.7 %all-to-all-start = ((bf16[16,32,256]{2,1,0:T(8,128)(2,1)}), bf16[16,32,256]{2,1,0:T(8,128)(2,1)S(1)}, u32[]{:S(2)}, u32[]{:S(2)}) async-start(bf16[16,32,256]{2,1,0:T(8,128)(2,1)} %shard_map.96), calls=%async_computation | async-start | bytes 524288 | tf_op jit(solution)/shard_map/all_to_all | solution.py:416
  42.6 2.1 %slice.4 = bf16[4,336,256]{2,1,0:T(8,128)(2,1)} slice(bf16[4,528,256]{2,1,0:T(8,128)(2,1)} %bitcast.30), slice={[0:4], [0:336], [0:256]} | slice | bytes 1376256 | tf_op jit(solution)/shard_map/slice | solution.py:543
  44.7 1.2 %collective-permute-start.8 = (bf16[4,336,256]{2,1,0:T(8,128)(2,1)}, bf16[4,336,256]{2,1,0:T(8,128)(2,1)}, u32[]{:S(2)}, u32[]{:S(2)}) collective-permute-start(bf16[4,336,256]{2,1,0:T(8,128)(2,1)} %slice.4), channel_id=1, source_target_pairs={{0,16},{16,0},{1,17},{17,1},{2,18},{18,2},{3,19},{19,3},{4,20},{20... | collective-permute-start | bytes 2064392 | tf_op jit(solution)/shard_map/ppermute | solution.py:543
  45.9 6.1 %all-to-all-done = bf16[16,32,256]{2,1,0:T(8,128)(2,1)S(1)} async-done(((bf16[16,32,256]{2,1,0:T(8,128)(2,1)}), bf16[16,32,256]{2,1,0:T(8,128)(2,1)S(1)}, u32[]{:S(2)}, u32[]{:S(2)}) %all-to-all-start) | async-done | bytes 262176 | tf_op jit(solution)/shard_map/all_to_all | solution.py:416
  52.1 1.3 %shard_map.97 = bf16[16,32,128]{2,1,0:T(8,128)(2,1)S(1)} custom-call(s32[7]{0:T(128)S(1)} %stack.31.marks_ref.marks, bf16[864,512]{1,0:T(8,128)(2,1)S(1)} %bitcast.27, bf16[112,256]{1,0:T(8,128)(2,1)S(1)} %get-tuple-element.28.refs_0_, bf16[112,256]{1,0:T(8,128)(2,1)S(1)} %collective-permute-done.5.refs_1_, ...), custom_call_target="tpu_custom_call" | custom-call | flops 226492416 | bytes 1376284 | tf_op jit(solution)/shard_map/pallas_call | solution.py:18
  53.4 10.3 %all_to_all.10.deeper = bf16[16,32,128]{2,1,0:T(8,128)(2,1)S(1)} all-to-all(bf16[16,32,128]{2,1,0:T(8,128)(2,1)S(1)} %shard_map.97), channel_id=1, replica_groups=mesh['rep'=2,'z'=4,'r'=4] {'z','r'}, dimensions={0} | all-to-all | bytes 262144 | tf_op jit(solution)/shard_map/all_to_all | solution.py:416
  63.7 2.9 %shard_map.98 = (bf16[128,256]{1,0:T(8,128)(2,1)S(1)}, bf16[128,256]{1,0:T(8,128)(2,1)S(1)}, bf16[128,256]{1,0:T(8,128)(2,1)S(1)}, bf16[128,256]{1,0:T(8,128)(2,1)S(1)}) custom-call(s32[7]{0:T(128)S(1)} %stack.31.marks_ref.marks, bf16[16,32,128]{2,1,0:T(8,128)(2,1)S(1)} %all_to_all.10.deeper, bf16[512,512]{1,0:T(8,128)(2,1)S(1)} %shard_map.93._.rise, ...), custom_call_target="tpu_custom_call" | custom-call | flops 905969664 | bytes 2654236 | tf_op jit(solution)/shard_map/pallas_call | solution.py:18
  66.6 0.5 collective-permute-start.10
  67.1 2.4 %collective-permute-start.11 = (bf16[128,256]{1,0:T(8,128)(2,1)S(1)}, bf16[128,256]{1,0:T(8,128)(2,1)S(1)}, u32[]{:S(2)}, u32[]{:S(2)}) collective-permute-start(bf16[128,256]{1,0:T(8,128)(2,1)S(1)} %get-tuple-element.36), channel_id=1, source_target_pairs={{0,3},{1,2},{2,1},{3,0},{4,7},{5,6},{6,5},{7,4},{8,11},{9,10},{10,... | collective-permute-start | bytes 196616 | tf_op jit(solution)/shard_map/ppermute | solution.py:421
  69.5 0.3 collective-permute-done.10.refs_2_
  69.8 2.5 %collective-permute-done.11.refs_3_ = bf16[128,256]{1,0:T(8,128)(2,1)S(1)} collective-permute-done((bf16[128,256]{1,0:T(8,128)(2,1)S(1)}, bf16[128,256]{1,0:T(8,128)(2,1)S(1)}, u32[]{:S(2)}, u32[]{:S(2)}) %collective-permute-start.11) | collective-permute-done | bytes 65568 | tf_op jit(solution)/shard_map/ppermute | solution.py:421
  72.3 1.1 %shard_map.99 = bf16[1024,128]{1,0:T(8,128)(2,1)} custom-call(bf16[128,256]{1,0:T(8,128)(2,1)S(1)} %get-tuple-element.33.refs_0_, bf16[128,256]{1,0:T(8,128)(2,1)S(1)} %collective-permute-done.9.refs_1_, bf16[128,256]{1,0:T(8,128)(2,1)S(1)} %collective-permute-done.10.refs_2_, bf16[128,256]{1,0:T(8,128)(2,1)S(1)} %collective-permute-done.11.refs_3_, ...), custom_call_target="tpu_custom_call" | custom-call | flops 67108864 | bytes 786432 | tf_op jit(solution)/shard_map/pallas_call | solution.py:18
  (27 shorter events, 0.1 us)
Async XLA Ops:
  6.5 36.1 %all-gather.3.cloned.1.call-start = ((), (), s32[]{:S(2)}) async-start(), calls=%async_computation.2 | async-start | bytes 1351680 | tf_op jit(solution)/shard_map/all_gather | solution.py:470
  6.5 9.8 %copy-start.2 = (bf16[3,3,3,128,128]{4,3,2,1,0:T(8,128)(2,1)S(1)}, bf16[3,3,3,128,128]{4,3,2,1,0:T(8,128)(2,1)}, u32[]{:S(2)}) copy-start(bf16[3,3,3,128,128]{4,3,2,1,0:T(8,128)(2,1)} %param.10) | copy-start | bytes 2654212
  8.7 9.6 %collective-permute-start = (bf16[3,16,16,128]{3,2,1,0:T(8,128)(2,1)}, bf16[3,16,16,128]{3,2,1,0:T(8,128)(2,1)S(1)}, u32[]{:S(2)}, u32[]{:S(2)}) collective-permute-start(bf16[3,16,16,128]{3,2,1,0:T(8,128)(2,1)} %get-tuple-element.21), channel_id=1, source_target_pairs={{1,2},{3,4},{5,6},{7,8},{9,10},{11,12},{13,14},{2,1},{4,3},{6,5},{... | collective-permute-start | bytes 589832 | tf_op jit(solution)/shard_map/ppermute | solution.py:466
  13.2 5.0 %collective-permute-start.1 = (bf16[3,16,16,128]{3,2,1,0:T(8,128)(2,1)}, bf16[3,16,16,128]{3,2,1,0:T(8,128)(2,1)S(1)}, u32[]{:S(2)}, u32[]{:S(2)}) collective-permute-start(bf16[3,16,16,128]{3,2,1,0:T(8,128)(2,1)} %get-tuple-element.22), channel_id=1, source_target_pairs={{0,1},{1,0},{2,3},{3,2},{4,5},{5,4},{6,7},{7,6},{8,9},{9,8},{10,11... | collective-permute-start | bytes 589832 | tf_op jit(solution)/shard_map/ppermute | solution.py:467
  13.4 1.6 %copy-start = (bf16[2,2,2,512,256]{4,3,2,1,0:T(8,128)(2,1)S(1)}, bf16[2,2,2,512,256]{4,3,2,1,0:T(8,128)(2,1)}, u32[]{:S(2)}) copy-start(bf16[2,2,2,512,256]{4,3,2,1,0:T(8,128)(2,1)} %param.14) | copy-start | bytes 6291460
  15.0 1.3 %copy-start.7 = (bf16[4,16,16,128]{3,2,1,0:T(8,128)(2,1)S(1)}, bf16[4,16,16,128]{3,2,1,0:T(8,128)(2,1)}, u32[]{:S(2)}) copy-start(bf16[4,16,16,128]{3,2,1,0:T(8,128)(2,1)} %volume.3) | copy-start | bytes 786436
  16.4 1.9 %copy-start.1 = (bf16[3,3,3,128,256]{4,3,2,1,0:T(8,128)(2,1)S(1)}, bf16[3,3,3,128,256]{4,3,2,1,0:T(8,128)(2,1)}, u32[]{:S(2)}) copy-start(bf16[3,3,3,128,256]{4,3,2,1,0:T(8,128)(2,1)} %param.11) | copy-start | bytes 5308420
  16.4 1.9 %copy-start.8 = (bf16[256,256]{1,0:T(8,128)(2,1)S(1)}, bf16[256,256]{1,0:T(8,128)(2,1)}, u32[]{:S(2)}) copy-start(bf16[256,256]{1,0:T(8,128)(2,1)} %constant.38.clone.order) | copy-start | bytes 393220
  18.3 18.8 %copy-start.5 = (bf16[3,3,3,256,32]{3,4,2,1,0:T(8,128)(2,1)S(1)}, bf16[3,3,3,256,32]{3,4,2,1,0:T(8,128)(2,1)}, u32[]{:S(2)}) copy-start(bf16[3,3,3,256,32]{3,4,2,1,0:T(8,128)(2,1)} %param.12) | copy-start | bytes 1327108
  21.1 30.9 %copy-start.3 = (bf16[3,3,3,512,32]{3,4,2,1,0:T(8,128)(2,1)S(1)}, bf16[3,3,3,512,32]{3,4,2,1,0:T(8,128)(2,1)}, u32[]{:S(2)}) copy-start(bf16[3,3,3,512,32]{3,4,2,1,0:T(8,128)(2,1)} %param.13) | copy-start | bytes 2654212
  21.2 4.3 %collective-permute-start.2 = (bf16[16,256]{1,0:T(8,128)(2,1)S(1)}, bf16[16,256]{1,0:T(8,128)(2,1)S(1)}, u32[]{:S(2)}, u32[]{:S(2)}) collective-permute-start(bf16[16,256]{1,0:T(8,128)(2,1)S(1)} %bitcast.32), channel_id=1, source_target_pairs={{0,4},{4,0},{8,12},{12,8},{1,5},{5,1},{9,13},{13,9},{2,6},{6,2},{1... | collective-permute-start | bytes 24584 | tf_op jit(solution)/shard_map/ppermute | solution.py:421
  23.2 4.5 %collective-permute-start.3 = (bf16[16,256]{1,0:T(8,128)(2,1)S(1)}, bf16[16,256]{1,0:T(8,128)(2,1)S(1)}, u32[]{:S(2)}, u32[]{:S(2)}) collective-permute-start(bf16[16,256]{1,0:T(8,128)(2,1)S(1)} %bitcast.33), channel_id=1, source_target_pairs={{0,8},{4,12},{8,0},{12,4},{1,9},{5,13},{9,1},{13,5},{2,10},{6,14},... | collective-permute-start | bytes 24584 | tf_op jit(solution)/shard_map/ppermute | solution.py:421
  25.5 4.5 %collective-permute-start.4 = (bf16[16,256]{1,0:T(8,128)(2,1)S(1)}, bf16[16,256]{1,0:T(8,128)(2,1)S(1)}, u32[]{:S(2)}, u32[]{:S(2)}) collective-permute-start(bf16[16,256]{1,0:T(8,128)(2,1)S(1)} %bitcast.34), channel_id=1, source_target_pairs={{0,12},{4,8},{8,4},{12,0},{1,13},{5,9},{9,5},{13,1},{2,14},{6,10},... | collective-permute-start | bytes 24584 | tf_op jit(solution)/shard_map/ppermute | solution.py:421
  30.5 3.0 %collective-permute-start.5 = (bf16[112,256]{1,0:T(8,128)(2,1)S(1)}, bf16[112,256]{1,0:T(8,128)(2,1)S(1)}, u32[]{:S(2)}, u32[]{:S(2)}) collective-permute-start(bf16[112,256]{1,0:T(8,128)(2,1)S(1)} %get-tuple-element.29), channel_id=1, source_target_pairs={{0,1},{1,0},{2,3},{3,2},{4,5},{5,4},{6,7},{7,6},{8,9},{9,8},{10,11... | collective-permute-start | bytes 172040 | tf_op jit(solution)/shard_map/ppermute | solution.py:421
  31.8 3.6 %collective-permute-start.6 = (bf16[112,256]{1,0:T(8,128)(2,1)S(1)}, bf16[112,256]{1,0:T(8,128)(2,1)S(1)}, u32[]{:S(2)}, u32[]{:S(2)}) collective-permute-start(bf16[112,256]{1,0:T(8,128)(2,1)S(1)} %get-tuple-element.30), channel_id=1, source_target_pairs={{0,2},{1,3},{2,0},{3,1},{4,6},{5,7},{6,4},{7,5},{8,10},{9,11},{10,... | collective-permute-start | bytes 172040 | tf_op jit(solution)/shard_map/ppermute | solution.py:421
  32.6 4.5 %collective-permute-start.7 = (bf16[112,256]{1,0:T(8,128)(2,1)S(1)}, bf16[112,256]{1,0:T(8,128)(2,1)S(1)}, u32[]{:S(2)}, u32[]{:S(2)}) collective-permute-start(bf16[112,256]{1,0:T(8,128)(2,1)S(1)} %get-tuple-element.31), channel_id=1, source_target_pairs={{0,3},{1,2},{2,1},{3,0},{4,7},{5,6},{6,5},{7,4},{8,11},{9,10},{10,... | collective-permute-start | bytes 172040 | tf_op jit(solution)/shard_map/ppermute | solution.py:421
  38.9 13.2 %all-to-all-start = ((bf16[16,32,256]{2,1,0:T(8,128)(2,1)}), bf16[16,32,256]{2,1,0:T(8,128)(2,1)S(1)}, u32[]{:S(2)}, u32[]{:S(2)}) async-start(bf16[16,32,256]{2,1,0:T(8,128)(2,1)} %shard_map.96), calls=%async_computation | async-start | bytes 524288 | tf_op jit(solution)/shard_map/all_to_all | solution.py:416
  42.6 21.1 %copy-start.6 = (bf16[2112,256]{1,0:T(8,128)(2,1)S(1)}, bf16[2112,256]{1,0:T(8,128)(2,1)}, u32[]{:S(2)}) copy-start(bf16[2112,256]{1,0:T(8,128)(2,1)} %all-gather.3.cloned.1.call-done) | copy-start | bytes 3244036
  44.7 19.0 %collective-permute-start.8 = (bf16[4,336,256]{2,1,0:T(8,128)(2,1)}, bf16[4,336,256]{2,1,0:T(8,128)(2,1)}, u32[]{:S(2)}, u32[]{:S(2)}) collective-permute-start(bf16[4,336,256]{2,1,0:T(8,128)(2,1)} %slice.4), channel_id=1, source_target_pairs={{0,16},{16,0},{1,17},{17,1},{2,18},{18,2},{3,19},{19,3},{4,20},{20... | collective-permute-start | bytes 2064392 | tf_op jit(solution)/shard_map/ppermute | solution.py:543
  53.3 19.0 %copy-start.4 = (bf16[2,2,2,256,128]{4,3,2,1,0:T(8,128)(2,1)S(1)}, bf16[2,2,2,256,128]{4,3,2,1,0:T(8,128)(2,1)}, u32[]{:S(2)}) copy-start(bf16[2,2,2,256,128]{4,3,2,1,0:T(8,128)(2,1)} %param.16) | copy-start | bytes 1572868
  66.6 3.2 %collective-permute-start.10 = (bf16[128,256]{1,0:T(8,128)(2,1)S(1)}, bf16[128,256]{1,0:T(8,128)(2,1)S(1)}, u32[]{:S(2)}, u32[]{:S(2)}) collective-permute-start(bf16[128,256]{1,0:T(8,128)(2,1)S(1)} %get-tuple-element.35), channel_id=1, source_target_pairs={{0,2},{1,3},{2,0},{3,1},{4,6},{5,7},{6,4},{7,5},{8,10},{9,11},{10,... | collective-permute-start | bytes 196616 | tf_op jit(solution)/shard_map/ppermute | solution.py:421
  67.1 5.2 %collective-permute-start.11 = (bf16[128,256]{1,0:T(8,128)(2,1)S(1)}, bf16[128,256]{1,0:T(8,128)(2,1)S(1)}, u32[]{:S(2)}, u32[]{:S(2)}) collective-permute-start(bf16[128,256]{1,0:T(8,128)(2,1)S(1)} %get-tuple-element.36), channel_id=1, source_target_pairs={{0,3},{1,2},{2,1},{3,0},{4,7},{5,6},{6,5},{7,4},{8,11},{9,10},{10,... | collective-permute-start | bytes 196616 | tf_op jit(solution)/shard_map/ppermute | solution.py:421
  69.5 2.9 %collective-permute-start.9 = (bf16[128,256]{1,0:T(8,128)(2,1)S(1)}, bf16[128,256]{1,0:T(8,128)(2,1)S(1)}, u32[]{:S(2)}, u32[]{:S(2)}) collective-permute-start(bf16[128,256]{1,0:T(8,128)(2,1)S(1)} %get-tuple-element.34), channel_id=1, source_target_pairs={{0,1},{1,0},{2,3},{3,2},{4,5},{5,4},{6,7},{7,6},{8,9},{9,8},{10,11... | collective-permute-start | bytes 196616 | tf_op jit(solution)/shard_map/ppermute | solution.py:421
Sparse Core Ops, SparseCore 0:
  8.9 31.1 all-gather.2

commit v4 on v3

--- a/solution.py
+++ b/solution.py
@@ -258,6 +258,28 @@
         out[dest] = deep
 
 
+def rider_stage(marks, *refs):
+    near, (out, blocks) = refs[:GROUP], refs[GROUP:]
+    by_rank(marks, near, blocks)
+    edges = [blocks[r, 32:48, :].astype(jnp.float32) for r in (0, GROUP - 1)]
+    riders = [
+        [
+            jnp.concatenate(
+                [
+                    pltpu.roll(edge[:, at // 128 * 128 : at // 128 * 128 + 128], (96 - at) % 128, 1)
+                    for at in (64 * r, 64 * r + 32)
+                ],
+                axis=0,
+            )
+            for r in range(GROUP)
+        ]
+        for edge in edges
+    ]
+    for e in range(2):
+        for r in range(GROUP):
+            out[e, r] = riders[e][r]
+
+
 def deeper_stage(near_count, marks, weights, *refs):
     near, (deep, out, blocks) = refs[:near_count], refs[near_count:]
     n, chans, _ = out.shape
@@ -265,23 +287,9 @@
     deeper = spread_taps(weights, deep[...], ((1,), (0,)), chans, voxels)
     lane = lax.broadcasted_iota(jnp.int32, (chans, 128), 1)
     planes = n // GROUP
-    ride = len(near) == GROUP
+    ride = len(near) == 1
     if ride:
-        by_rank(marks, near, blocks)
-        edges = [blocks[r, 32:48, :].astype(jnp.float32) for r in (0, GROUP - 1)]
-        riders = [
-            [
-                jnp.concatenate(
-                    [
-                        pltpu.roll(edge[:, at // 128 * 128 : at // 128 * 128 + 128], (96 - at) % 128, 1)
-                        for at in (64 * r, 64 * r + 32)
-                    ],
-                    axis=0,
-                )
-                for r in range(GROUP)
-            ]
-            for edge in edges
-        ]
+        riders = near[0]
     for p in range(planes):
         part = pltpu.roll(deeper, (16 - 64 * p) % voxels, 1)[:, :128]
         if p == 0:
@@ -291,7 +299,7 @@
         for r in range(GROUP):
             whole = part
             if ride:
-                rider = jnp.where(marks[3] < p, riders[1][r], riders[0][r])
+                rider = jnp.where(marks[3] < p, riders[1, r], riders[0, r])
                 whole = jnp.where(lane < 96, part, rider)
             out[GROUP * p + r] = whole.astype(jnp.bfloat16)
 
@@ -564,7 +572,10 @@
         swaps = (near_swap, far_swap)
     deep_whole = (exchange(deep, ALL).reshape(n * chans, voxels),)
 
-    riders = near if ride else ()
+    riders = ()
+    if ride:
+        shape = jax.ShapeDtypeStruct((2, GROUP, 32, 128), jnp.float32)
+        riders = (call(rider_stage, shape, [blocks], (marks, *near), 0, 16, scalars=1),)
     deeper = call(
         functools.partial(deeper_stage, len(riders)),
         bf16((n, chans, 128)),

time: 80.6 us -> 80.6 us (level)
    pallas_call x8 -> x9, Pallas kernels: 13.2 us -> 13.8 us  [call(): pl.pallas_call(kernel, out_shape=outs, in_specs=[pl.BlockSpec(memory_spac...]
where the time goes in v4:
time: 80.6 us; the launch traced here: 80.2 us
  starting transfers between devices  19.7 us (24%)
  waiting for transfers between devices  16.9 us (21%)
  Pallas kernels  16 us (20%)
  between operations  13.6 us (17%)
  blocking collectives  10.3 us (13%)
  local copies, waits for them, and re-layouts  3.82 us (5%)
    pallas_call x9, Pallas kernels, call(): pl.pallas_call(kernel, out_shape=outs, in_specs=[pl.BlockSpec(memory_spac...  13.8 us
    ppermute x9, waiting for transfers between devices, by_xor(): lax.ppermute(blocks[k], axis, swaps[k])  10.9 us
    all_to_all x1, blocking collectives, exchange(): lax.all_to_all(payload, axis, split_axis=0, concat_axis=0, tiled=True)  10.3 us
    ppermute x9, starting transfers between devices, by_xor(): lax.ppermute(blocks[k], axis, swaps[k])  10.2 us
    all_to_all x1, waiting for transfers between devices, exchange(): lax.all_to_all(payload, axis, split_axis=0, concat_axis=0, tiled=True)  5.49 us
    ppermute x1, starting transfers between devices, body(): off_chip = lax.ppermute(off_chip, ALL, pairs + [(j, i) for i, j in pairs])  4.54 us
    all_to_all x1, starting transfers between devices, exchange(): lax.all_to_all(payload, axis, split_axis=0, concat_axis=0, tiled=True)  3.66 us
    pallas_call x1, Pallas kernels, body(): pl.pallas_call(front_stage, out_shape=(halo, halo) + (bf16((528, 256)),)...  2.11 us
  transfers between devices with their start and end apart: 14, of which 8 were waited for; matrix products, arithmetic and copies ran while one was open for 3% of the time, Pallas kernels for 12%

profile of v4, /device:TPU:1, one launch (start us, length us, event | category | flops | bytes accessed | tf_op | source)
XLA Modules:
  0.0 80.2 jit_solution(6919383309594925182)
XLA Ops:
  6.5 2.1 %shard_map.91 = (bf16[3,16,16,128]{3,2,1,0:T(8,128)(2,1)}, bf16[3,16,16,128]{3,2,1,0:T(8,128)(2,1)}, bf16[528,256]{1,0:T(8,128)(2,1)}) custom-call(s32[1]{0:T(128)} %bitcast.4.odd, s32[1]{0:T(128)} %bitcast.1.rep, bf16[4,16,16,128]{3,2,1,0:T(8,128)(2,1)} %volume.3, bf16[864,256]{1,0:T(8,128)(2,1)} %bitcast.36), custom_call_target="tpu_custom_call" | custom-call | bytes 1000000 | tf_op jit(solution)/shard_map/pallas_call | solution.py:459
  8.7 4.5 %collective-permute-start = (bf16[3,16,16,128]{3,2,1,0:T(8,128)(2,1)}, bf16[3,16,16,128]{3,2,1,0:T(8,128)(2,1)S(1)}, u32[]{:S(2)}, u32[]{:S(2)}) collective-permute-start(bf16[3,16,16,128]{3,2,1,0:T(8,128)(2,1)} %get-tuple-element.21), channel_id=1, source_target_pairs={{1,2},{3,4},{5,6},{7,8},{9,10},{11,12},{13,14},{2,1},{4,3},{6,5},{... | collective-permute-start | bytes 589832 | tf_op jit(solution)/shard_map/ppermute | solution.py:474
  13.3 0.1 stack.31.marks_ref.marks
  13.4 1.6 %copy-done = bf16[2,2,2,512,256]{4,3,2,1,0:T(8,128)(2,1)S(1)} copy-done((bf16[2,2,2,512,256]{4,3,2,1,0:T(8,128)(2,1)S(1)}, bf16[2,2,2,512,256]{4,3,2,1,0:T(8,128)(2,1)}, u32[]{:S(2)}) %copy-start) | copy-done | bytes 2097176
  15.0 1.3 %shard_map.93._.rise = bf16[512,512]{1,0:T(8,128)(2,1)S(1)} custom-call(s32[7]{0:T(128)S(1)} %stack.31.marks_ref.marks, bf16[8,512,256]{2,1,0:T(8,128)(2,1)S(1)} %bitcast.22), custom_call_target="tpu_custom_call" | custom-call | flops 134217728 | bytes 2097180 | tf_op jit(solution)/shard_map/pallas_call | solution.py:18
  16.4 1.4 %shard_map.92.own = f32[4,256,256]{2,1,0:T(8,128)S(1)} custom-call(bf16[4,16,16,128]{3,2,1,0:T(8,128)(2,1)S(1)} %copy-done.7, bf16[3,1152,128]{2,1,0:T(8,128)(2,1)S(1)} %bitcast.25), custom_call_target="tpu_custom_call" | custom-call | flops 1207959552 | bytes 1146880 | tf_op jit(solution)/shard_map/pallas_call | solution.py:18
  17.8 0.4 collective-permute-done.off_chip
  18.3 2.9 %shard_map.94 = (bf16[1,16,256]{2,1,0:T(8,128)(2,1)S(1)}, bf16[48,256]{1,0:T(8,128)(2,1)S(1)}, bf16[48,256]{1,0:T(8,128)(2,1)S(1)}, bf16[48,256]{1,0:T(8,128)(2,1)S(1)}, bf16[48,256]{1,0:T(8,128)(2,1)S(1)}) custom-call(s32[7]{0:T(128)S(1)} %stack.31.marks_ref.marks, bf16[3,16,16,128]{3,2,1,0:T(8,128)(2,1)S(1)} %collective-permute-done.off_chip, ...), custom_call_target="tpu_custom_call" | custom-call | flops 1207959552 | bytes 4227100 | tf_op jit(solution)/shard_map/pallas_call | solution.py:18
  21.2 2.0 %collective-permute-start.2 = (bf16[16,256]{1,0:T(8,128)(2,1)S(1)}, bf16[16,256]{1,0:T(8,128)(2,1)S(1)}, u32[]{:S(2)}, u32[]{:S(2)}) collective-permute-start(bf16[16,256]{1,0:T(8,128)(2,1)S(1)} %bitcast.32), channel_id=1, source_target_pairs={{0,4},{4,0},{8,12},{12,8},{1,5},{5,1},{9,13},{13,9},{2,6},{6,2},{1... | collective-permute-start | bytes 24584 | tf_op jit(solution)/shard_map/ppermute | solution.py:429
  23.2 2.3 %collective-permute-start.3 = (bf16[16,256]{1,0:T(8,128)(2,1)S(1)}, bf16[16,256]{1,0:T(8,128)(2,1)S(1)}, u32[]{:S(2)}, u32[]{:S(2)}) collective-permute-start(bf16[16,256]{1,0:T(8,128)(2,1)S(1)} %bitcast.33), channel_id=1, source_target_pairs={{0,8},{4,12},{8,0},{12,4},{1,9},{5,13},{9,1},{13,5},{2,10},{6,14},... | collective-permute-start | bytes 24584 | tf_op jit(solution)/shard_map/ppermute | solution.py:429
  25.5 2.2 %collective-permute-done.3.refs_2_ = bf16[16,256]{1,0:T(8,128)(2,1)S(1)} collective-permute-done((bf16[16,256]{1,0:T(8,128)(2,1)S(1)}, bf16[16,256]{1,0:T(8,128)(2,1)S(1)}, u32[]{:S(2)}, u32[]{:S(2)}) %collective-permute-start.3) | collective-permute-done | bytes 8224 | tf_op jit(solution)/shard_map/ppermute | solution.py:429
  27.7 2.3 %collective-permute-done.4.refs_3_ = bf16[16,256]{1,0:T(8,128)(2,1)S(1)} collective-permute-done((bf16[16,256]{1,0:T(8,128)(2,1)S(1)}, bf16[16,256]{1,0:T(8,128)(2,1)S(1)}, u32[]{:S(2)}, u32[]{:S(2)}) %collective-permute-start.4) | collective-permute-done | bytes 8224 | tf_op jit(solution)/shard_map/ppermute | solution.py:429
  30.0 0.6 shard_map.95
  30.5 1.3 %collective-permute-start.5 = (bf16[112,256]{1,0:T(8,128)(2,1)S(1)}, bf16[112,256]{1,0:T(8,128)(2,1)S(1)}, u32[]{:S(2)}, u32[]{:S(2)}) collective-permute-start(bf16[112,256]{1,0:T(8,128)(2,1)S(1)} %get-tuple-element.29), channel_id=1, source_target_pairs={{0,1},{1,0},{2,3},{3,2},{4,5},{5,4},{6,7},{7,6},{8,9},{9,8},{10,11... | collective-permute-start | bytes 172040 | tf_op jit(solution)/shard_map/ppermute | solution.py:429
  31.8 0.8 %collective-permute-start.6 = (bf16[112,256]{1,0:T(8,128)(2,1)S(1)}, bf16[112,256]{1,0:T(8,128)(2,1)S(1)}, u32[]{:S(2)}, u32[]{:S(2)}) collective-permute-start(bf16[112,256]{1,0:T(8,128)(2,1)S(1)} %get-tuple-element.30), channel_id=1, source_target_pairs={{0,2},{1,3},{2,0},{3,1},{4,6},{5,7},{6,4},{7,5},{8,10},{9,11},{10,... | collective-permute-start | bytes 172040 | tf_op jit(solution)/shard_map/ppermute | solution.py:429
  32.6 0.9 %collective-permute-start.7 = (bf16[112,256]{1,0:T(8,128)(2,1)S(1)}, bf16[112,256]{1,0:T(8,128)(2,1)S(1)}, u32[]{:S(2)}, u32[]{:S(2)}) collective-permute-start(bf16[112,256]{1,0:T(8,128)(2,1)S(1)} %get-tuple-element.31), channel_id=1, source_target_pairs={{0,3},{1,2},{2,1},{3,0},{4,7},{5,6},{6,5},{7,4},{8,11},{9,10},{10,... | collective-permute-start | bytes 172040 | tf_op jit(solution)/shard_map/ppermute | solution.py:429
  33.5 1.9 %collective-permute-done.6.refs_2_ = bf16[112,256]{1,0:T(8,128)(2,1)S(1)} collective-permute-done((bf16[112,256]{1,0:T(8,128)(2,1)S(1)}, bf16[112,256]{1,0:T(8,128)(2,1)S(1)}, u32[]{:S(2)}, u32[]{:S(2)}) %collective-permute-start.6) | collective-permute-done | bytes 57376 | tf_op jit(solution)/shard_map/ppermute | solution.py:429
  35.4 1.7 %collective-permute-done.7.refs_3_ = bf16[112,256]{1,0:T(8,128)(2,1)S(1)} collective-permute-done((bf16[112,256]{1,0:T(8,128)(2,1)S(1)}, bf16[112,256]{1,0:T(8,128)(2,1)S(1)}, u32[]{:S(2)}, u32[]{:S(2)}) %collective-permute-start.7) | collective-permute-done | bytes 57376 | tf_op jit(solution)/shard_map/ppermute | solution.py:429
  37.1 1.8 %shard_map.97 = bf16[16,32,256]{2,1,0:T(8,128)(2,1)} custom-call(s32[7]{0:T(128)S(1)} %stack.31.marks_ref.marks, bf16[864,256]{1,0:T(8,128)(2,1)S(1)} %bitcast.29, bf16[112,256]{1,0:T(8,128)(2,1)S(1)} %get-tuple-element.28.refs_0_, bf16[112,256]{1,0:T(8,128)(2,1)S(1)} %collective-permute-done.5.refs_1_, bf16[112,256]{1,0:T(8,128)(2,1)S(1)} %collective-permute-done.6.refs_2_, ...), custom_call_target="tpu_custom_call" | custom-call | flops 113246208 | bytes 671772 | tf_op jit(solution)/shard_map/pallas_call | solution.py:18
  38.9 3.7 %all-to-all-start = ((bf16[16,32,256]{2,1,0:T(8,128)(2,1)}), bf16[16,32,256]{2,1,0:T(8,128)(2,1)S(1)}, u32[]{:S(2)}, u32[]{:S(2)}) async-start(bf16[16,32,256]{2,1,0:T(8,128)(2,1)} %shard_map.97), calls=%async_computation | async-start | bytes 524288 | tf_op jit(solution)/shard_map/all_to_all | solution.py:424
  42.6 2.1 %slice.4 = bf16[4,336,256]{2,1,0:T(8,128)(2,1)} slice(bf16[4,528,256]{2,1,0:T(8,128)(2,1)} %bitcast.30), slice={[0:4], [0:336], [0:256]} | slice | bytes 1376256 | tf_op jit(solution)/shard_map/slice | solution.py:551
  44.7 1.2 %collective-permute-start.8 = (bf16[4,336,256]{2,1,0:T(8,128)(2,1)}, bf16[4,336,256]{2,1,0:T(8,128)(2,1)}, u32[]{:S(2)}, u32[]{:S(2)}) collective-permute-start(bf16[4,336,256]{2,1,0:T(8,128)(2,1)} %slice.4), channel_id=1, source_target_pairs={{0,16},{16,0},{1,17},{17,1},{2,18},{18,2},{3,19},{19,3},{4,20},{20... | collective-permute-start | bytes 2064392 | tf_op jit(solution)/shard_map/ppermute | solution.py:551
  45.9 0.6 shard_map.96.refs_0_
  46.6 5.5 %all-to-all-done = bf16[16,32,256]{2,1,0:T(8,128)(2,1)S(1)} async-done(((bf16[16,32,256]{2,1,0:T(8,128)(2,1)}), bf16[16,32,256]{2,1,0:T(8,128)(2,1)S(1)}, u32[]{:S(2)}, u32[]{:S(2)}) %all-to-all-start) | async-done | bytes 262176 | tf_op jit(solution)/shard_map/all_to_all | solution.py:424
  52.1 1.3 %shard_map.98 = bf16[16,32,128]{2,1,0:T(8,128)(2,1)S(1)} custom-call(s32[7]{0:T(128)S(1)} %stack.31.marks_ref.marks, bf16[864,512]{1,0:T(8,128)(2,1)S(1)} %bitcast.27, f32[2,4,32,128]{3,2,1,0:T(8,128)S(1)} %shard_map.96.refs_0_, bf16[512,256]{1,0:T(8,128)(2,1)S(1)} %bitcast.24), custom_call_target="tpu_custom_call" | custom-call | flops 226492416 | bytes 1277980 | tf_op jit(solution)/shard_map/pallas_call | solution.py:18
  53.4 10.3 %all_to_all.10.deeper = bf16[16,32,128]{2,1,0:T(8,128)(2,1)S(1)} all-to-all(bf16[16,32,128]{2,1,0:T(8,128)(2,1)S(1)} %shard_map.98), channel_id=1, replica_groups=mesh['rep'=2,'z'=4,'r'=4] {'z','r'}, dimensions={0} | all-to-all | bytes 262144 | tf_op jit(solution)/shard_map/all_to_all | solution.py:424
  63.7 2.9 %shard_map.99 = (bf16[128,256]{1,0:T(8,128)(2,1)S(1)}, bf16[128,256]{1,0:T(8,128)(2,1)S(1)}, bf16[128,256]{1,0:T(8,128)(2,1)S(1)}, bf16[128,256]{1,0:T(8,128)(2,1)S(1)}) custom-call(s32[7]{0:T(128)S(1)} %stack.31.marks_ref.marks, bf16[16,32,128]{2,1,0:T(8,128)(2,1)S(1)} %all_to_all.10.deeper, bf16[512,512]{1,0:T(8,128)(2,1)S(1)} %shard_map.93._.rise, ...), custom_call_target="tpu_custom_call" | custom-call | flops 905969664 | bytes 2654236 | tf_op jit(solution)/shard_map/pallas_call | solution.py:18
  66.6 0.5 collective-permute-start.10
  67.1 2.4 %collective-permute-start.11 = (bf16[128,256]{1,0:T(8,128)(2,1)S(1)}, bf16[128,256]{1,0:T(8,128)(2,1)S(1)}, u32[]{:S(2)}, u32[]{:S(2)}) collective-permute-start(bf16[128,256]{1,0:T(8,128)(2,1)S(1)} %get-tuple-element.36), channel_id=1, source_target_pairs={{0,3},{1,2},{2,1},{3,0},{4,7},{5,6},{6,5},{7,4},{8,11},{9,10},{10,... | collective-permute-start | bytes 196616 | tf_op jit(solution)/shard_map/ppermute | solution.py:429
  69.5 0.3 collective-permute-done.10.refs_2_
  69.8 2.5 %collective-permute-done.11.refs_3_ = bf16[128,256]{1,0:T(8,128)(2,1)S(1)} collective-permute-done((bf16[128,256]{1,0:T(8,128)(2,1)S(1)}, bf16[128,256]{1,0:T(8,128)(2,1)S(1)}, u32[]{:S(2)}, u32[]{:S(2)}) %collective-permute-start.11) | collective-permute-done | bytes 65568 | tf_op jit(solution)/shard_map/ppermute | solution.py:429
  72.3 1.1 %shard_map.100 = bf16[1024,128]{1,0:T(8,128)(2,1)} custom-call(bf16[128,256]{1,0:T(8,128)(2,1)S(1)} %get-tuple-element.33.refs_0_, bf16[128,256]{1,0:T(8,128)(2,1)S(1)} %collective-permute-done.9.refs_1_, bf16[128,256]{1,0:T(8,128)(2,1)S(1)} %collective-permute-done.10.refs_2_, bf16[128,256]{1,0:T(8,128)(2,1)S(1)} %collective-permute-done.11.refs_3_, ...), custom_call_target="tpu_custom_call" | custom-call | flops 67108864 | bytes 786432 | tf_op jit(solution)/shard_map/pallas_call | solution.py:18
  (28 shorter events, 0.2 us)
Async XLA Ops:
  6.5 36.1 %all-gather.3.cloned.1.call-start = ((), (), s32[]{:S(2)}) async-start(), calls=%async_computation.2 | async-start | bytes 1351680 | tf_op jit(solution)/shard_map/all_gather | solution.py:478
  6.5 9.8 %copy-start.2 = (bf16[3,3,3,128,128]{4,3,2,1,0:T(8,128)(2,1)S(1)}, bf16[3,3,3,128,128]{4,3,2,1,0:T(8,128)(2,1)}, u32[]{:S(2)}) copy-start(bf16[3,3,3,128,128]{4,3,2,1,0:T(8,128)(2,1)} %param.10) | copy-start | bytes 2654212
  8.7 9.6 %collective-permute-start = (bf16[3,16,16,128]{3,2,1,0:T(8,128)(2,1)}, bf16[3,16,16,128]{3,2,1,0:T(8,128)(2,1)S(1)}, u32[]{:S(2)}, u32[]{:S(2)}) collective-permute-start(bf16[3,16,16,128]{3,2,1,0:T(8,128)(2,1)} %get-tuple-element.21), channel_id=1, source_target_pairs={{1,2},{3,4},{5,6},{7,8},{9,10},{11,12},{13,14},{2,1},{4,3},{6,5},{... | collective-permute-start | bytes 589832 | tf_op jit(solution)/shard_map/ppermute | solution.py:474
  13.2 5.0 %collective-permute-start.1 = (bf16[3,16,16,128]{3,2,1,0:T(8,128)(2,1)}, bf16[3,16,16,128]{3,2,1,0:T(8,128)(2,1)S(1)}, u32[]{:S(2)}, u32[]{:S(2)}) collective-permute-start(bf16[3,16,16,128]{3,2,1,0:T(8,128)(2,1)} %get-tuple-element.22), channel_id=1, source_target_pairs={{0,1},{1,0},{2,3},{3,2},{4,5},{5,4},{6,7},{7,6},{8,9},{9,8},{10,11... | collective-permute-start | bytes 589832 | tf_op jit(solution)/shard_map/ppermute | solution.py:475
  13.4 1.6 %copy-start = (bf16[2,2,2,512,256]{4,3,2,1,0:T(8,128)(2,1)S(1)}, bf16[2,2,2,512,256]{4,3,2,1,0:T(8,128)(2,1)}, u32[]{:S(2)}) copy-start(bf16[2,2,2,512,256]{4,3,2,1,0:T(8,128)(2,1)} %param.14) | copy-start | bytes 6291460
  15.0 1.3 %copy-start.7 = (bf16[4,16,16,128]{3,2,1,0:T(8,128)(2,1)S(1)}, bf16[4,16,16,128]{3,2,1,0:T(8,128)(2,1)}, u32[]{:S(2)}) copy-start(bf16[4,16,16,128]{3,2,1,0:T(8,128)(2,1)} %volume.3) | copy-start | bytes 786436
  16.4 1.9 %copy-start.1 = (bf16[3,3,3,128,256]{4,3,2,1,0:T(8,128)(2,1)S(1)}, bf16[3,3,3,128,256]{4,3,2,1,0:T(8,128)(2,1)}, u32[]{:S(2)}) copy-start(bf16[3,3,3,128,256]{4,3,2,1,0:T(8,128)(2,1)} %param.11) | copy-start | bytes 5308420
  16.4 1.9 %copy-start.8 = (bf16[256,256]{1,0:T(8,128)(2,1)S(1)}, bf16[256,256]{1,0:T(8,128)(2,1)}, u32[]{:S(2)}) copy-start(bf16[256,256]{1,0:T(8,128)(2,1)} %constant.38.clone.order) | copy-start | bytes 393220
  18.3 18.8 %copy-start.5 = (bf16[3,3,3,256,32]{3,4,2,1,0:T(8,128)(2,1)S(1)}, bf16[3,3,3,256,32]{3,4,2,1,0:T(8,128)(2,1)}, u32[]{:S(2)}) copy-start(bf16[3,3,3,256,32]{3,4,2,1,0:T(8,128)(2,1)} %param.12) | copy-start | bytes 1327108
  21.1 30.9 %copy-start.3 = (bf16[3,3,3,512,32]{3,4,2,1,0:T(8,128)(2,1)S(1)}, bf16[3,3,3,512,32]{3,4,2,1,0:T(8,128)(2,1)}, u32[]{:S(2)}) copy-start(bf16[3,3,3,512,32]{3,4,2,1,0:T(8,128)(2,1)} %param.13) | copy-start | bytes 2654212
  21.2 4.3 %collective-permute-start.2 = (bf16[16,256]{1,0:T(8,128)(2,1)S(1)}, bf16[16,256]{1,0:T(8,128)(2,1)S(1)}, u32[]{:S(2)}, u32[]{:S(2)}) collective-permute-start(bf16[16,256]{1,0:T(8,128)(2,1)S(1)} %bitcast.32), channel_id=1, source_target_pairs={{0,4},{4,0},{8,12},{12,8},{1,5},{5,1},{9,13},{13,9},{2,6},{6,2},{1... | collective-permute-start | bytes 24584 | tf_op jit(solution)/shard_map/ppermute | solution.py:429
  23.2 4.5 %collective-permute-start.3 = (bf16[16,256]{1,0:T(8,128)(2,1)S(1)}, bf16[16,256]{1,0:T(8,128)(2,1)S(1)}, u32[]{:S(2)}, u32[]{:S(2)}) collective-permute-start(bf16[16,256]{1,0:T(8,128)(2,1)S(1)} %bitcast.33), channel_id=1, source_target_pairs={{0,8},{4,12},{8,0},{12,4},{1,9},{5,13},{9,1},{13,5},{2,10},{6,14},... | collective-permute-start | bytes 24584 | tf_op jit(solution)/shard_map/ppermute | solution.py:429
  25.5 4.5 %collective-permute-start.4 = (bf16[16,256]{1,0:T(8,128)(2,1)S(1)}, bf16[16,256]{1,0:T(8,128)(2,1)S(1)}, u32[]{:S(2)}, u32[]{:S(2)}) collective-permute-start(bf16[16,256]{1,0:T(8,128)(2,1)S(1)} %bitcast.34), channel_id=1, source_target_pairs={{0,12},{4,8},{8,4},{12,0},{1,13},{5,9},{9,5},{13,1},{2,14},{6,10},... | collective-permute-start | bytes 24584 | tf_op jit(solution)/shard_map/ppermute | solution.py:429
  30.5 3.0 %collective-permute-start.5 = (bf16[112,256]{1,0:T(8,128)(2,1)S(1)}, bf16[112,256]{1,0:T(8,128)(2,1)S(1)}, u32[]{:S(2)}, u32[]{:S(2)}) collective-permute-start(bf16[112,256]{1,0:T(8,128)(2,1)S(1)} %get-tuple-element.29), channel_id=1, source_target_pairs={{0,1},{1,0},{2,3},{3,2},{4,5},{5,4},{6,7},{7,6},{8,9},{9,8},{10,11... | collective-permute-start | bytes 172040 | tf_op jit(solution)/shard_map/ppermute | solution.py:429
  31.8 3.6 %collective-permute-start.6 = (bf16[112,256]{1,0:T(8,128)(2,1)S(1)}, bf16[112,256]{1,0:T(8,128)(2,1)S(1)}, u32[]{:S(2)}, u32[]{:S(2)}) collective-permute-start(bf16[112,256]{1,0:T(8,128)(2,1)S(1)} %get-tuple-element.30), channel_id=1, source_target_pairs={{0,2},{1,3},{2,0},{3,1},{4,6},{5,7},{6,4},{7,5},{8,10},{9,11},{10,... | collective-permute-start | bytes 172040 | tf_op jit(solution)/shard_map/ppermute | solution.py:429
  32.6 4.5 %collective-permute-start.7 = (bf16[112,256]{1,0:T(8,128)(2,1)S(1)}, bf16[112,256]{1,0:T(8,128)(2,1)S(1)}, u32[]{:S(2)}, u32[]{:S(2)}) collective-permute-start(bf16[112,256]{1,0:T(8,128)(2,1)S(1)} %get-tuple-element.31), channel_id=1, source_target_pairs={{0,3},{1,2},{2,1},{3,0},{4,7},{5,6},{6,5},{7,4},{8,11},{9,10},{10,... | collective-permute-start | bytes 172040 | tf_op jit(solution)/shard_map/ppermute | solution.py:429
  38.9 13.2 %all-to-all-start = ((bf16[16,32,256]{2,1,0:T(8,128)(2,1)}), bf16[16,32,256]{2,1,0:T(8,128)(2,1)S(1)}, u32[]{:S(2)}, u32[]{:S(2)}) async-start(bf16[16,32,256]{2,1,0:T(8,128)(2,1)} %shard_map.97), calls=%async_computation | async-start | bytes 524288 | tf_op jit(solution)/shard_map/all_to_all | solution.py:424
  42.6 21.1 %copy-start.6 = (bf16[2112,256]{1,0:T(8,128)(2,1)S(1)}, bf16[2112,256]{1,0:T(8,128)(2,1)}, u32[]{:S(2)}) copy-start(bf16[2112,256]{1,0:T(8,128)(2,1)} %all-gather.3.cloned.1.call-done) | copy-start | bytes 3244036
  44.7 19.0 %collective-permute-start.8 = (bf16[4,336,256]{2,1,0:T(8,128)(2,1)}, bf16[4,336,256]{2,1,0:T(8,128)(2,1)}, u32[]{:S(2)}, u32[]{:S(2)}) collective-permute-start(bf16[4,336,256]{2,1,0:T(8,128)(2,1)} %slice.4), channel_id=1, source_target_pairs={{0,16},{16,0},{1,17},{17,1},{2,18},{18,2},{3,19},{19,3},{4,20},{20... | collective-permute-start | bytes 2064392 | tf_op jit(solution)/shard_map/ppermute | solution.py:551
  53.3 19.0 %copy-start.4 = (bf16[2,2,2,256,128]{4,3,2,1,0:T(8,128)(2,1)S(1)}, bf16[2,2,2,256,128]{4,3,2,1,0:T(8,128)(2,1)}, u32[]{:S(2)}) copy-start(bf16[2,2,2,256,128]{4,3,2,1,0:T(8,128)(2,1)} %param.16) | copy-start | bytes 1572868
  66.6 3.2 %collective-permute-start.10 = (bf16[128,256]{1,0:T(8,128)(2,1)S(1)}, bf16[128,256]{1,0:T(8,128)(2,1)S(1)}, u32[]{:S(2)}, u32[]{:S(2)}) collective-permute-start(bf16[128,256]{1,0:T(8,128)(2,1)S(1)} %get-tuple-element.35), channel_id=1, source_target_pairs={{0,2},{1,3},{2,0},{3,1},{4,6},{5,7},{6,4},{7,5},{8,10},{9,11},{10,... | collective-permute-start | bytes 196616 | tf_op jit(solution)/shard_map/ppermute | solution.py:429
  67.1 5.2 %collective-permute-start.11 = (bf16[128,256]{1,0:T(8,128)(2,1)S(1)}, bf16[128,256]{1,0:T(8,128)(2,1)S(1)}, u32[]{:S(2)}, u32[]{:S(2)}) collective-permute-start(bf16[128,256]{1,0:T(8,128)(2,1)S(1)} %get-tuple-element.36), channel_id=1, source_target_pairs={{0,3},{1,2},{2,1},{3,0},{4,7},{5,6},{6,5},{7,4},{8,11},{9,10},{10,... | collective-permute-start | bytes 196616 | tf_op jit(solution)/shard_map/ppermute | solution.py:429
  69.5 2.9 %collective-permute-start.9 = (bf16[128,256]{1,0:T(8,128)(2,1)S(1)}, bf16[128,256]{1,0:T(8,128)(2,1)S(1)}, u32[]{:S(2)}, u32[]{:S(2)}) collective-permute-start(bf16[128,256]{1,0:T(8,128)(2,1)S(1)} %get-tuple-element.34), channel_id=1, source_target_pairs={{0,1},{1,0},{2,3},{3,2},{4,5},{5,4},{6,7},{7,6},{8,9},{9,8},{10,11... | collective-permute-start | bytes 196616 | tf_op jit(solution)/shard_map/ppermute | solution.py:429
Sparse Core Ops, SparseCore 0:
  8.9 31.1 all-gather.2
